TPU v7x, 256 devices: a whole 4x4x8 slice. The times are simulated.
256 devices in a mesh: lat: 64 (over z, y_lo, x), lon: 4 (over y_hi, core).
Axes of the slice: x: 4, y: 4 (y_hi: 2, y_lo: 2; y = y_hi * 2 + y_lo), z: 8, core: 2. Of those that a mesh axis runs over, the one named last changes fastest.
Arguments:
- field: bfloat16 [256, 768, 256], P('lat', 'lon'), may hold values from -6 to 6
- cotangent: bfloat16 [256, 768, 256], P('lat', 'lon'), may hold values from -6 to 6
- legendre: bfloat16 [16, 384, 256], P(None, None, 'lat'), as said below
- cycle_weight: float32 [256], P('lat'), may hold values from 0.5 to 1.5
- support_tap: int32 [256, 18], replicated, may hold values from 0 to 8
- support_basis: int32 [256, 18], replicated, may hold values from 0 to 3
- support_weight: float32 [256, 18], replicated, may hold values from 0.5 to 2
- filter_weight: bfloat16 [4, 256, 256], replicated, may hold values from -0.1875 to 0.1875
- spectral_weight: bfloat16 [256, 256], replicated, may hold values from -0.375 to 0.375
- spectral_gain: bfloat16 [384, 256], P('lat', 'lon'), may hold values from 0.5 to 2
Outputs:
- output: bfloat16 [256, 768, 256], P('lat', 'lon')
- grad_field: bfloat16 [256, 768, 256], P('lat', 'lon')
- grad_filter: float32 [4, 256, 256], replicated
- grad_spectral: float32 [256, 256], P(None, 'lon')
Inputs may be any that keep to these rules, and one draw needn't show every extreme that they name: legendre[t, l, i] is zero wherever l < t, and lies within -4 / sqrt(256) to 4 / sqrt(256).
All inputs are finite; a program needn't handle non-finite values.
Results may differ from a plain program's by a relative error of at most 0.019.
Values may be sent and summed in bfloat16 or wider, within the bound.
A program may use at most 64 MiB of HBM per device.

v0:
```python
import math

import jax
import jax.numpy as jnp
from jax import lax
from jax.sharding import PartitionSpec as P

LONGITUDES = 768
DEGREES = 384
ORDERS = 16
BASIS_COUNT = 4


def with_halo(x, sides, width, wrap):
    for axis, dim in sides:
        devices, length = (lax.axis_size(axis), x.shape[dim])
        up = [(i, (i + 1) % devices) for i in range(devices if wrap else devices - 1)]
        down = [(j, i) for i, j in up]
        last = lax.slice_in_dim(x, length - width, length, axis=dim)
        initial = lax.slice_in_dim(x, 0, width, axis=dim)
        before = lax.ppermute(last, axis, up)
        after = lax.ppermute(initial, axis, down)
        x = jnp.concatenate([before, x, after], axis=dim)
    return x


def tap_table(support_tap, support_basis, support_weight):
    tap_onehot = (support_tap[:, :, None] == jnp.arange(9, dtype=jnp.int32)[None, None, :]).astype(
        jnp.float32
    )
    basis_onehot = (
        support_basis[:, :, None] == jnp.arange(BASIS_COUNT, dtype=jnp.int32)[None, None, :]
    ).astype(jnp.float32)
    table = jnp.einsum(
        "ist,isk->itk",
        tap_onehot * support_weight[:, :, None],
        basis_onehot,
        precision=lax.Precision.HIGHEST,
    )
    return table.astype(jnp.bfloat16)


def trig_table(scale):
    longitude = jnp.arange(LONGITUDES, dtype=jnp.int32)
    order = jnp.arange(ORDERS, dtype=jnp.int32)
    turns = longitude[:, None] * order[None, :] % LONGITUDES
    angle = turns.astype(jnp.float32) * (2.0 * math.pi / LONGITUDES)
    return (jnp.stack([jnp.cos(angle), jnp.sin(angle)], axis=1) * scale).astype(jnp.bfloat16)


def extend_rims(values):
    wider = with_halo(values, (("lon", 1),), 1, True)
    return with_halo(wider, (("lat", 0),), 1, False)


def filter_rows(extended, tap_rows):
    count = extended.shape[0] - 2
    width = extended.shape[1] - 2
    shifted = jnp.stack(
        [
            extended[north : north + count, east : east + width]
            for north in range(3)
            for east in range(3)
        ],
        axis=1,
    )
    return jnp.einsum(
        "atk,atjc->akjc", tap_rows, shifted, preferred_element_type=jnp.float32
    ).astype(jnp.bfloat16)


def spread_back(spread_near, tap_near, count, width):
    summed = jnp.zeros((count, width, spread_near.shape[3]), jnp.float32)
    for north in range(3):
        for east in range(3):
            row_first = 2 - north
            column_first = 2 - east
            weights = tap_near[row_first : row_first + count, 3 * north + east]
            values = spread_near[row_first : row_first + count, column_first : column_first + width]
            summed = summed + jnp.einsum(
                "ak,ajkc->ajc", weights, values, preferred_element_type=jnp.float32
            )
    return summed


def spectral_pass(values, table_in, table_out, before, after, legendre, gain, mixing, adjoint):
    cycle_count, width, channels = values.shape
    orders = legendre.shape[0]
    degrees_here = gain.shape[0]
    quarter = gain.shape[1]
    channel_start = lax.axis_index("lon") * quarter
    regrouped = lax.all_to_all(values, "lon", split_axis=2, concat_axis=1, tiled=True)
    modes = jnp.einsum("ajc,jrm->amrc", regrouped, table_in, preferred_element_type=jnp.float32)
    modes = (modes * before[:, None, None, None]).astype(jnp.bfloat16)
    flat_modes = modes.reshape(cycle_count, orders, 2 * quarter)
    degree_block = legendre
    spectrum = lax.psum_scatter(
        jnp.einsum("mla,amx->lmx", degree_block, flat_modes, preferred_element_type=jnp.float32),
        "lat",
        scatter_dimension=0,
        tiled=True,
    )
    spectrum = spectrum.astype(jnp.bfloat16).reshape(degrees_here, orders, 2, quarter)
    gain_wide = gain.astype(jnp.float32)[:, None, None, :]
    if adjoint:
        local = (gain_wide * spectrum.astype(jnp.float32)).astype(jnp.bfloat16)
    else:
        local = spectrum
    whole = lax.all_gather(local, "lon", axis=3, tiled=True)
    if adjoint:
        rows_used = lax.dynamic_slice_in_dim(mixing, channel_start, quarter, 0)
        mixed = jnp.einsum(
            "lmrf,cf->lmrc", whole, rows_used, preferred_element_type=jnp.float32
        ).astype(jnp.bfloat16)
    else:
        columns_used = lax.dynamic_slice_in_dim(mixing, channel_start, quarter, 1)
        mixed = (
            gain_wide
            * jnp.einsum("lmrc,cf->lmrf", whole, columns_used, preferred_element_type=jnp.float32)
        ).astype(jnp.bfloat16)
    flat_mixed = mixed.reshape(degrees_here, orders, 2 * quarter)
    degree_block = legendre
    cycle_sums = jnp.einsum(
        "mla,lmx->amx",
        degree_block,
        lax.all_gather(flat_mixed, "lat", axis=0, tiled=True),
        preferred_element_type=jnp.float32,
    )
    cycle_modes = cycle_sums.astype(jnp.bfloat16).reshape(cycle_count, orders, 2, quarter)
    spatial = jnp.einsum(
        "amrc,jrm->ajc", cycle_modes, table_out, preferred_element_type=jnp.float32
    )
    spatial = (spatial * after[:, None, None]).astype(jnp.bfloat16)
    spatial = lax.all_to_all(spatial, "lon", split_axis=1, concat_axis=2, tiled=True)
    return (spatial, whole, local)


def per_device(
    field,
    cotangent,
    legendre,
    cycle_weight,
    support_tap,
    support_basis,
    support_weight,
    filter_weight,
    spectral_weight,
    spectral_gain,
):
    cycle_count, width, channels = field.shape
    cycle_start = lax.axis_index("lat") * cycle_count
    tap_all = tap_table(support_tap, support_basis, support_weight)
    tap_padded = jnp.pad(tap_all, ((1, 1), (0, 0), (0, 0)))
    tap_own = lax.dynamic_slice_in_dim(tap_all, cycle_start, cycle_count, 0)
    tap_near = lax.dynamic_slice_in_dim(tap_padded, cycle_start, cycle_count + 2, 0)
    filtered = filter_rows(extend_rims(field), tap_own)
    filter_out = jnp.einsum(
        "akjc,kcf->ajf", filtered, filter_weight, preferred_element_type=jnp.float32
    )
    hidden = (field.astype(jnp.float32) + filter_out).astype(jnp.bfloat16)
    analysis_table = trig_table(LONGITUDES ** (-0.5))
    synthesis_table = trig_table((2 * ORDERS) ** (-0.5))
    ones = jnp.ones_like(cycle_weight)
    spatial, spectrum_whole, ignored = spectral_pass(
        hidden,
        analysis_table,
        synthesis_table,
        cycle_weight,
        ones,
        legendre,
        spectral_gain,
        spectral_weight,
        False,
    )
    output = (hidden.astype(jnp.float32) + spatial.astype(jnp.float32)).astype(jnp.bfloat16)
    back_spatial, unused, scaled = spectral_pass(
        cotangent,
        synthesis_table,
        analysis_table,
        ones,
        cycle_weight,
        legendre,
        spectral_gain,
        spectral_weight,
        True,
    )
    grad_hidden = (cotangent.astype(jnp.float32) + back_spatial.astype(jnp.float32)).astype(
        jnp.bfloat16
    )
    spectral_term = jnp.einsum(
        "lmrc,lmrf->cf", spectrum_whole, scaled, preferred_element_type=jnp.float32
    ) * (2 * ORDERS * DEGREES) ** (-0.5)
    grad_spectral = lax.psum(spectral_term, "lat")
    spread = jnp.einsum(
        "ajf,kcf->ajkc", grad_hidden, filter_weight, preferred_element_type=jnp.float32
    ).astype(jnp.bfloat16)
    spread_near = extend_rims(spread)
    back_filter = spread_back(spread_near, tap_near, cycle_count, width)
    grad_field = (grad_hidden.astype(jnp.float32) + back_filter).astype(jnp.bfloat16)
    grid_scale = (cycle_count * lax.axis_size("lat") * LONGITUDES) ** (-0.5)
    filter_term = (
        jnp.einsum("akjc,ajf->kcf", filtered, grad_hidden, preferred_element_type=jnp.float32)
        * grid_scale
    )
    grad_filter = lax.psum(filter_term, ("lat", "lon"))
    return (output, grad_field, grad_filter, grad_spectral)


def solution(mesh):
    placed = (
        P("lat", "lon", None),
        P("lat", "lon", None),
        P(None, None, "lat"),
        P("lat"),
        P(),
        P(),
        P(),
        P(),
        P(),
        P("lat", "lon"),
    )
    return jax.shard_map(
        per_device,
        mesh=mesh,
        in_specs=placed,
        out_specs=(P("lat", "lon", None), P("lat", "lon", None), P(), P(None, "lon")),
        check_vma=False,
    )
```

profile of v0, /device:TPU:1, one launch (start us, length us, event | category | flops | bytes accessed | tf_op | source)
XLA Modules:
  0.0 2060.8 jit_solution(2623669714929116673)
XLA Ops:
  9.3 6.7 all-to-all-start.2
  16.2 9.3 all-to-all-done.2
  26.8 2.2 convolution_bitcast_fusion
  29.1 3.6 copy.295
  35.1 2.7 fusion.48
  39.2 2.4 collective-permute-start.2
  44.5 2.9 collective-permute-done.3
  57.0 29.0 %stack.47 = bf16[4,9,192,256]{3,1,2,0:T(8,128)(2,1)} concatenate(bf16[4,1,192,256]{3,1,2,0:T(2,128)(2,1)} %copy.264, bf16[4,1,192,256]{3,1,2,0:T(2,128)(2,1)} %copy.265, bf16[4,1,192,256]{3,1,2,0:T(2,128)(2,1)} %copy.266, bf16[4,1,192,256]{3,1,2,0:T(2,128)(2,1)S(1)} %copy.267, bf16[4,1,192,256]{3,1,2,0:T(2,128)(2,1)S(1)} %copy.268, bf16[4,1,192,256]{3,1,2,0:T(2,128)(2,1)S(1)} %copy.269, ...), dimensions={1} | concatenate | bytes 7077888 | tf_op jit(solution)/shard_map/stack | solution.py:59
  86.0 3.8 convolution_convert_fusion
  91.8 16.9 all_to_all.54
  110.2 2.3 convolution_bitcast_fusion.1
  112.5 3.6 copy.279
  116.7 186.6 %reduce-scatter.5.cloned.1.call-done = f32[6,16,128]{2,1,0:T(8,128)} async-done(((f32[384,16,128]{2,1,0:T(8,128)}), f32[6,16,128]{2,1,0:T(8,128)}) %reduce-scatter.5.cloned.1.call-update) | async-done | bytes 49168 | tf_op jit(solution)/shard_map/reduce_scatter | solution.py:97
  304.4 59.6 %all_gather.14 = bf16[6,16,2,256]{1,2,0,3:T(2,128)(2,1)S(1)} all-gather(bf16[6,16,2,64]{1,2,0,3:T(2,128)(2,1)S(1)} %copy.297), channel_id=1, replica_groups=mesh['lat'=64,'lon'=4] {'lon'}, dimensions={3}, use_global_device_ids=true | all-gather | bytes 122880 | tf_op jit(solution)/shard_map/all_gather | solution.py:109
  365.2 255.7 %reduce-scatter.3.cloned.1.call-done = f32[6,16,128]{2,1,0:T(8,128)} async-done(((f32[384,16,128]{2,1,0:T(8,128)}), f32[6,16,128]{2,1,0:T(8,128)}) %reduce-scatter.3.cloned.1.call-update) | async-done | bytes 49168 | tf_op jit(solution)/shard_map/reduce_scatter | solution.py:97
  621.9 60.7 %all_gather.12 = bf16[6,16,2,256]{1,2,0,3:T(2,128)(2,1)S(1)} all-gather(bf16[6,16,2,64]{1,2,0,3:T(2,128)(2,1)S(1)} %copy.280), channel_id=1, replica_groups=mesh['lat'=64,'lon'=4] {'lon'}, dimensions={3}, use_global_device_ids=true | all-gather | bytes 122880 | tf_op jit(solution)/shard_map/all_gather | solution.py:109
  691.3 231.7 %all-gather.5.cloned.1.call-done = bf16[384,16,128]{2,1,0:T(8,128)(2,1)} async-done(((bf16[6,16,128]{2,1,0:T(8,128)(2,1)}), bf16[384,16,128]{2,1,0:T(8,128)(2,1)}) %all-gather.5.cloned.1.call-update) | async-done | bytes 1572880 | tf_op jit(solution)/shard_map/all_gather | solution.py:126
  927.3 49.9 %all-to-all-start.3 = ((bf16[4,2,24576]{2,1,0:T(2,128)(2,1)}), bf16[4,2,24576]{2,1,0:T(2,128)(2,1)S(1)}, u32[]{:S(2)}, u32[]{:S(2)}) async-start(bf16[4,2,24576]{2,1,0:T(2,128)(2,1)} %reshape.175), calls=%async_computation.5 | async-start | bytes 786432 | tf_op jit(solution)/shard_map/all_to_all | solution.py:134
  977.1 243.9 %all-gather.3.cloned.1.call-done = bf16[384,16,128]{2,1,0:T(8,128)(2,1)} async-done(((bf16[6,16,128]{2,1,0:T(8,128)(2,1)}), bf16[384,16,128]{2,1,0:T(8,128)(2,1)}) %all-gather.3.cloned.1.call-update) | async-done | bytes 1572880 | tf_op jit(solution)/shard_map/all_gather | solution.py:126
  1225.2 49.9 %all-to-all-start.1 = ((bf16[4,2,24576]{2,1,0:T(2,128)(2,1)}), bf16[4,2,24576]{2,1,0:T(2,128)(2,1)}, u32[]{:S(2)}, u32[]{:S(2)}) async-start(bf16[4,2,24576]{2,1,0:T(2,128)(2,1)} %reshape.173), calls=%async_computation.2 | async-start | bytes 786432 | tf_op jit(solution)/shard_map/all_to_all | solution.py:134
  1279.6 3.2 collective-permute-start.4
  1290.3 4.8 collective-permute-start.7
  1297.3 2.2 fusion.16
  1301.6 3.5 copy.335
  1310.4 2.8 pad_maximum_fusion
  1319.1 2.2 fusion.14
  1333.3 3.7 copy.341
  1337.0 3.5 copy.344
  1340.6 4.6 fusion.70
  1347.1 417.5 %all-reduce.6.cloned.1.call-done = f32[256,64]{0,1:T(8,128)} async-done(((f32[256,64]{0,1:T(8,128)}), f32[256,64]{0,1:T(8,128)}) %all-reduce.6.cloned.1.call-update) | async-done | bytes 65552 | tf_op jit(solution)/shard_map/psum | solution.py:193
  1764.6 286.2 %all-reduce.4.cloned.1.call-done = f32[4,256,256]{2,1,0:T(8,128)} async-done(((f32[4,256,256]{2,1,0:T(8,128)}), f32[4,256,256]{2,1,0:T(8,128)}) %all-reduce.4.cloned.1.call-update) | async-done | bytes 1048592 | tf_op jit(solution)/shard_map/psum | solution.py:205
  2050.9 2.3 copy.411
  (183 shorter events, 86.0 us)
Async XLA Ops:
  7.2 83.8 %copy-start = (bf16[4,256,256]{2,1,0:T(8,128)(2,1)S(1)}, bf16[4,256,256]{2,1,0:T(8,128)(2,1)}, u32[]{:S(2)}) copy-start(bf16[4,256,256]{2,1,0:T(8,128)(2,1)} %param.17) | copy-start | bytes 1572868
  9.3 16.2 all-to-all-start.2
  16.0 287.3 %reduce-scatter.5.cloned.1.call-start = ((), (), s32[]{:S(2)}) async-start(), calls=%async_computation.8 | async-start | bytes 3194880 | tf_op jit(solution)/shard_map/reduce_scatter | solution.py:97
  16.2 10.6 copy-start.12
  32.7 2.3 copy-start.17
  32.7 588.1 %reduce-scatter.3.cloned.1.call-start = ((), (), s32[]{:S(2)}) async-start(), calls=%async_computation.6 | async-start | bytes 3194880 | tf_op jit(solution)/shard_map/reduce_scatter | solution.py:97
  33.7 4.7 collective-permute-start
  34.6 4.5 collective-permute-start.1
  39.2 5.3 collective-permute-start.2
  41.6 5.8 collective-permute-start.3
  91.5 17.7 copy-start.8
  116.1 247.9 %copy-start.14 = (bf16[256,256]{1,0:T(8,128)(2,1)S(1)}, bf16[256,256]{1,0:T(8,128)(2,1)}, u32[]{:S(2)}) copy-start(bf16[256,256]{1,0:T(8,128)(2,1)} %param.18) | copy-start | bytes 393220
  116.1 806.9 %all-gather.5.cloned.1.call-start = ((), (), s32[]{:S(2)}) async-start(), calls=%async_computation.9 | async-start | bytes 1597440 | tf_op jit(solution)/shard_map/all_gather | solution.py:126
  364.3 320.4 %copy-start.7 = (bf16[4,192,256]{2,1,0:T(8,128)(2,1)S(1)}, bf16[4,192,256]{2,1,0:T(8,128)(2,1)}, u32[]{:S(2)}) copy-start(bf16[4,192,256]{2,1,0:T(8,128)(2,1)} %param.11) | copy-start | bytes 1179652
  365.1 855.8 %all-gather.3.cloned.1.call-start = ((), (), s32[]{:S(2)}) async-start(), calls=%async_computation.7 | async-start | bytes 1597440 | tf_op jit(solution)/shard_map/all_gather | solution.py:126
  621.9 63.1 %copy-start.11 = (bf16[256,9,4]{1,2,0:T(4,128)(2,1)S(1)}, bf16[256,9,4]{1,2,0:T(4,128)(2,1)}, u32[]{:S(2)}) copy-start(bf16[256,9,4]{1,2,0:T(4,128)(2,1)} %fusion.48) | copy-start | bytes 55300
  684.3 1080.4 %all-reduce.6.cloned.1.call-start = ((), (), s32[]{:S(2)}) async-start(), calls=%async_computation.11 | async-start | bytes 131072 | tf_op jit(solution)/shard_map/psum | solution.py:193
  927.3 298.0 %all-to-all-start.3 = ((bf16[4,2,24576]{2,1,0:T(2,128)(2,1)}), bf16[4,2,24576]{2,1,0:T(2,128)(2,1)S(1)}, u32[]{:S(2)}, u32[]{:S(2)}) async-start(bf16[4,2,24576]{2,1,0:T(2,128)(2,1)} %reshape.175), calls=%async_computation.5 | async-start | bytes 786432 | tf_op jit(solution)/shard_map/all_to_all | solution.py:134
  1225.2 79.9 %all-to-all-start.1 = ((bf16[4,2,24576]{2,1,0:T(2,128)(2,1)}), bf16[4,2,24576]{2,1,0:T(2,128)(2,1)}, u32[]{:S(2)}, u32[]{:S(2)}) async-start(bf16[4,2,24576]{2,1,0:T(2,128)(2,1)} %reshape.173), calls=%async_computation.2 | async-start | bytes 786432 | tf_op jit(solution)/shard_map/all_to_all | solution.py:134
  1275.2 775.7 %all-reduce.4.cloned.1.call-start = ((), (), s32[]{:S(2)}) async-start(), calls=%async_computation.10 | async-start | bytes 2097152 | tf_op jit(solution)/shard_map/psum | solution.py:205
  1277.8 5.0 copy-start.28
  1279.6 6.5 collective-permute-start.4
  1282.8 5.1 collective-permute-start.5
  1289.0 21.4 %collective-permute-start.6 = (bf16[1,194,4,256]{3,1,2,0:T(8,128)(2,1)}, bf16[1,194,4,256]{3,1,2,0:T(8,128)(2,1)}, u32[]{:S(2)}, u32[]{:S(2)}) collective-permute-start(bf16[1,194,4,256]{3,1,2,0:T(8,128)(2,1)} %get-tuple-element.49), channel_id=1, source_target_pairs={{4,0},{8,4},{12,8},{16,12},{20,16},{24,20},{28,24},{32,28},{36,32}... | collective-permute-start | bytes 1191944 | tf_op jit(solution)/shard_map/ppermute | solution.py:22
  1290.3 5.7 copy-start.27
  1290.3 20.1 collective-permute-start.7
  1306.7 2.9 copy-start.9
  1327.6 3.8 copy-start.10
  1333.3 7.3 copy-start.3
  1333.3 7.3 copy-start.4
  1340.5 713.2 %copy-start.1 = (bf16[4,256,256]{2,1,0:T(8,128)(2,1)S(1)}, bf16[4,256,256]{2,1,0:T(8,128)(2,1)}, u32[]{:S(2)}) copy-start(bf16[4,256,256]{2,1,0:T(8,128)(2,1)} %param.17) | copy-start | bytes 1572868
  1764.6 288.5 %copy-start.13 = (f32[256,64]{0,1:T(8,128)S(1)}, f32[256,64]{0,1:T(8,128)}, u32[]{:S(2)}) copy-start(f32[256,64]{0,1:T(8,128)} %all-reduce.6.cloned.1.call-done) | copy-start | bytes 196612
  (14 other events, 20.2 us)
Sparse Core Ops, SparseCore 0:
  32.8 270.3 reduce-scatter.4
  305.9 314.8 reduce-scatter.2
  623.2 299.7 all-gather.4
  924.6 296.2 all-gather.2
  1224.0 540.5 all-reduce.5
  1770.8 279.9 all-reduce.3
where the time goes:
time: 2070 us; the launch traced here: 2060 us
  waiting for transfers between devices  1640 us (79%)
  blocking collectives  137 us (7%)
  starting transfers between devices  121 us (6%)
  local copies, waits for them, and re-layouts  102 us (5%)
  matrix products  36.1 us (2%)
    all_gather x2, waiting for transfers between devices, spectral_pass(): lax.all_gather(flat_mixed, 'lat', axis=0, tiled=True)  476 us
    reduce_scatter x2, waiting for transfers between devices, spectral_pass(): lax.psum_scatter(jnp.einsum('mla,amx->lmx', degree_block, flat_modes, pre...  442 us
    psum x1, waiting for transfers between devices, per_device(): grad_spectral = lax.psum(spectral_term, 'lat')  417 us
    psum x1, waiting for transfers between devices, per_device(): grad_filter = lax.psum(filter_term, ('lat', 'lon'))  286 us
    all_gather x2, blocking collectives, spectral_pass(): whole = lax.all_gather(local, 'lon', axis=3, tiled=True)  120 us
    all_to_all x2, starting transfers between devices, spectral_pass(): lax.all_to_all(spatial, 'lon', split_axis=1, concat_axis=2, tiled=True)  99.8 us
  transfers between devices with their start and end apart: 17, of which 10 were waited for; matrix products, arithmetic and copies ran while one was open for 7% of the time, Pallas kernels for 0%

commit v1 on v0

v1 whole, which is shorter than its diff:
```python
import math

import jax
import jax.numpy as jnp
import numpy as np
from jax import lax
from jax.experimental import pallas as pl
from jax.experimental.pallas import tpu as pltpu
from jax.sharding import PartitionSpec as P

LATITUDES = 256
LONGITUDES = 768
DEGREES = 384
ORDERS = 16
BASIS_COUNT = 4
LAT = 64
LON = 4
WIDTH = LONGITUDES // LON
WIDE = WIDTH + 32
ROWS = 1280
PIECE = 80
MESH = pl.DeviceIdType.MESH
BF = jnp.bfloat16
F32 = jnp.float32


def trig_tables():
    longitude = np.arange(LONGITUDES)
    order = np.arange(ORDERS)
    angle = (longitude[:, None] * order[None, :] % LONGITUDES) * (2.0 * math.pi / LONGITUDES)
    table = np.stack([np.cos(angle), np.sin(angle)], axis=2).reshape(LONGITUDES, 2 * ORDERS)
    both = np.stack([table * LONGITUDES ** (-0.5), table * (2 * ORDERS) ** (-0.5)])
    both = both.astype(np.float32)
    where = np.arange(LON)[:, None] * WIDTH + np.arange(-16, WIDTH + 16)[None, :]
    wide = both[:, where % LONGITUDES].transpose(1, 0, 2, 3)
    across = wide[:, :, 16 : 16 + WIDTH].transpose(0, 1, 3, 2)
    return wide, across


def whole_wait(ref, sem):
    pltpu.make_async_copy(ref, ref, sem).wait()


def unpack_constants():
    pick = np.zeros((3, 128, 256), np.float32)
    gain_pick = np.zeros((2, 48, 256), np.float32)
    for dev in range(8):
        for block in range(3):
            for group in range(4):
                for cycle in range(4):
                    pick[block, dev * 16 + group * 4 + cycle, dev * 32 + block * 4 + cycle] = 1.0
        for half in range(2):
            for degree in range(6):
                gain_pick[half, dev * 6 + degree, dev * 32 + 16 + half * 6 + degree] = 1.0
    return pick, gain_pick


def block_kernel(
    tap_ref,
    cycle_weight_ref,
    field_ref,
    cot_ref,
    legendre_ref,
    gain_ref,
    mixing_ref,
    filter_ref,
    pick_ref,
    gain_pick_ref,
    wide_ref,
    across_ref,
    out_ref,
    grad_ref,
    grad_filter_ref,
    grad_spectral_ref,
    field_wide,
    cot_wide,
    grad_wide,
    band,
    band_back,
    filtered,
    filtered_t,
    hidden,
    grad_own,
    partial,
    partial_src,
    lon_buf,
    gain_buf,
    table_src,
    table_buf,
    mode_src,
    mode_buf,
    rep,
    rep_t,
    gain_all,
    spec,
    scaled_s,
    mixed,
    back_src,
    cycle_buf,
    cycle_wide,
    fore_cycles,
    near_cycles,
    terms,
    core_src,
    core_buf,
    plane_src,
    plane_buf,
    z_buf,
    whole_buf,
    sem,
    lon_sem,
    near_sem,
):
    a = lax.axis_index("lat")
    b = lax.axis_index("lon")
    half = lax.div(a, 32)
    slot = lax.rem(a, 32)
    x = lax.rem(a, 4)
    y_lo = lax.rem(lax.div(a, 4), 2)
    z = lax.div(a, 8)
    core = lax.rem(b, 2)
    y_hi = lax.div(b, 2)
    place = (y_hi * 2 + y_lo) * 4 + x
    other_core = y_hi * 2 + 1 - core
    north, south = lax.rem(a + LAT - 1, LAT), lax.rem(a + 1, LAT)
    west, east = lax.rem(b + LON - 1, LON), lax.rem(b + 1, LON)
    barrier = pltpu.get_barrier_semaphore()

    def plane_peer(g):
        py, px = lax.div(g, 4), lax.rem(g, 4)
        return (z * 8 + lax.rem(py, 2) * 4 + px, lax.div(py, 2) * 2 + core)

    def z_peer(g):
        return (g * 8 + y_lo * 4 + x, b)

    def greet(device):
        pl.semaphore_signal(barrier, inc=1, device_id=device, device_id_type=MESH)

    def greet_lat(d, carry):
        greet((lax.rem(a + d, LAT), b))
        return carry

    def greet_far(d, carry):
        g = lax.rem(lax.rem(place, 8) + d, 8)
        greet((z * 8 + g, (1 - y_hi) * 2 + core))
        return carry

    for d in range(1, LON):
        greet((a, lax.rem(b + d, LON)))
    for lat in (north, south):
        for lon in (west, east):
            greet((lat, lon))
    lax.fori_loop(1, 8, greet_far, 0)
    lax.fori_loop(1, LAT, greet_lat, 0)

    def send(src, dst, send_sem, recv_sem, device):
        copy = pltpu.make_async_remote_copy(
            src_ref=src,
            dst_ref=dst,
            send_sem=send_sem,
            recv_sem=recv_sem,
            device_id=device,
            device_id_type=MESH,
        )
        copy.start()
        return copy

    field_wide[1:5, 16 : 16 + WIDTH, :] = field_ref[...]
    cot_wide[1:5, 16 : 16 + WIDTH, :] = cot_ref[...]

    def pack_partial(which, table, rows):
        for i in range(4):
            sums = jnp.dot(across_ref[b, table], rows[i], preferred_element_type=F32)
            for h in range(2):
                partial[which, pl.ds(h * 4 + i, 32, stride=8), :] = sums[:, h * 128 : h * 128 + 128]
        partial_src[which] = partial[which].astype(BF)

    pack_partial(1, 1, cot_ref)
    pl.semaphore_wait(barrier, LAT - 1 + LON - 1 + 4 + 7)

    def send_rims(src, dst, send_sem, recv_sem):
        last, first = pl.ds(WIDTH - 16, 16), pl.ds(0, 16)
        left, right, middle = pl.ds(0, 16), pl.ds(WIDTH + 16, 16), pl.ds(16, WIDTH)
        send(src.at[3], dst.at[0, middle, :], send_sem, recv_sem, (south, b))
        send(src.at[0], dst.at[5, middle, :], send_sem, recv_sem, (north, b))
        inner = pl.ds(1, 4)
        send(src.at[:, last, :], dst.at[inner, left, :], send_sem, recv_sem, (a, east))
        send(src.at[:, first, :], dst.at[inner, right, :], send_sem, recv_sem, (a, west))
        send(src.at[3, last, :], dst.at[0, left, :], send_sem, recv_sem, (south, east))
        send(src.at[3, first, :], dst.at[0, right, :], send_sem, recv_sem, (south, west))
        send(src.at[0, last, :], dst.at[5, left, :], send_sem, recv_sem, (north, east))
        send(src.at[0, first, :], dst.at[5, right, :], send_sem, recv_sem, (north, west))

    def rims_size(dst):
        return dst.at[pl.ds(0, 3), pl.ds(0, WIDTH), :]

    def to_lon(src, buf, kind):
        return [
            send(
                src,
                buf.at[d - 1],
                lon_sem.at[kind, 0, d - 1],
                lon_sem.at[kind, 1, d - 1],
                (a, lax.rem(b + d, LON)),
            )
            for d in range(1, LON)
        ]

    send_rims(field_ref, field_wide, sem.at[0], sem.at[1])
    gain_copies = to_lon(gain_ref, gain_buf, 0)
    back_copies = to_lon(partial_src.at[1], lon_buf.at[1], 1)

    diagonal = lax.broadcasted_iota(jnp.int32, (96, 128), 1)
    diagonal = diagonal - lax.broadcasted_iota(jnp.int32, (96, 128), 0) - 15
    inside_north = jnp.where(a == 0, 0.0, 1.0)
    inside_south = jnp.where(a == LAT - 1, 0.0, 1.0)

    def make_band(dst, i, adjoint):
        for p in range(3):
            for k in range(BASIS_COUNT):
                block = jnp.zeros((96, 128), F32)
                for q in range(3):
                    if adjoint:
                        value = tap_ref[i + p, (8 - 3 * p - q) * BASIS_COUNT + k]
                    else:
                        value = tap_ref[i + 1, (3 * p + q) * BASIS_COUNT + k]
                        if i == 0 and p == 0:
                            value = value * inside_north
                        if i == 3 and p == 2:
                            value = value * inside_south
                    block = jnp.where(diagonal == q, value, block)
                dst[i, k * 96 : k * 96 + 96, p * 128 : p * 128 + 128] = block.astype(BF)

    for i in range(4):
        make_band(band, i, False)

    for copy in gain_copies:
        copy.wait()
    gain_row = gain_ref[...].astype(F32)
    for d in range(LON - 1):
        gain_row = gain_row + gain_buf[d].astype(F32)
    gain_row = gain_row.astype(BF)
    for t in range(ORDERS):
        table_src[t, 0:16, :] = legendre_ref[t]
        table_src[t, 16:32, :] = gain_row

    def send_table(d, carry):
        to = lax.rem(a + d, LAT)
        src = table_src.at[lax.div(lax.rem(to, 32), 2)]
        send(src, table_buf.at[a], sem.at[2], sem.at[3], (to, b))
        return carry

    lax.fori_loop(1, LAT, send_table, 0)
    own_table = pltpu.make_async_copy(
        table_src.at[lax.div(slot, 2)], table_buf.at[a], sem.at[4]
    )
    own_table.start()

    def stencil(src, bands, i, block):
        near = jnp.concatenate([src[i + p, block * 96 : block * 96 + 128, :] for p in range(3)])
        return jnp.dot(bands[i], near, preferred_element_type=F32).astype(BF)

    whole_wait(rims_size(field_wide), sem.at[1])
    for i in range(4):
        for block in range(2):
            sums = stencil(field_wide, band, i, block)
            first = i * WIDTH + block * 96
            for k in range(BASIS_COUNT):
                filtered[first : first + 96, k * 256 : k * 256 + 256] = sums[k * 96 : k * 96 + 96]
        own = slice(i * WIDTH, i * WIDTH + WIDTH)
        mix = jnp.dot(filtered[own, :], filter_ref[...], preferred_element_type=F32)
        hidden[i] = (field_ref[i].astype(F32) + mix).astype(BF)
    pack_partial(0, 0, hidden)
    fore_copies = to_lon(partial_src.at[0], lon_buf.at[0], 2)
    send_rims(cot_ref, cot_wide, sem.at[5], sem.at[6])

    own_table.wait()
    whole_wait(table_buf.at[pl.ds(0, LAT - 1)], sem.at[3])
    for chunk in range(8):
        packed = table_buf[chunk * 8 : chunk * 8 + 8].reshape(256, 128)
        for block in range(3):
            rows = jnp.dot(pick_ref[block], packed, preferred_element_type=F32)
            rep[chunk * 128 : chunk * 128 + 128, block * 128 : block * 128 + 128] = rows.astype(BF)
            rep_t[block * 128 : block * 128 + 128, chunk * 128 : chunk * 128 + 128] = rows.T.astype(
                BF
            )
        for side in range(2):
            rows = jnp.dot(gain_pick_ref[side], packed, preferred_element_type=F32)
            gain_all[chunk * 48 : chunk * 48 + 48, side * 128 : side * 128 + 128] = rows

    for copy in back_copies + fore_copies:
        copy.wait()
    cycle = lax.rem(lax.broadcasted_iota(jnp.int32, (8, 128), 0), 4)
    weight = jnp.zeros((8, 128), F32)
    for i in range(4):
        weight = jnp.where(cycle == i, cycle_weight_ref[i], weight)
    for part in range(4):
        rows = pl.ds(part * 64, 64)
        totals = []
        for which in range(2):
            total = partial_src[which, rows, :].astype(F32)
            for d in range(LON - 1):
                total = total + lon_buf[which, d, rows, :].astype(F32)
            totals.append(total.reshape(8, 8, 128))
        total = jnp.concatenate([totals[0] * weight[None], totals[1]], axis=1)
        mode_src[pl.ds(part * 128, 128), :] = total.reshape(128, 128).astype(BF)

    def tile(index):
        return pl.ds(pl.multiple_of(index * 16, 16), 16)

    def send_modes(d, carry):
        to = lax.rem(a + d, LAT)
        src = mode_src.at[tile(lax.rem(to, 32)), :]
        send(src, mode_buf.at[tile(a), :], sem.at[7], sem.at[8], (to, b))
        return carry

    lax.fori_loop(1, LAT, send_modes, 0)
    own_modes = pltpu.make_async_copy(
        mode_src.at[tile(slot), :], mode_buf.at[tile(a), :], sem.at[9]
    )
    own_modes.start()

    for k in range(BASIS_COUNT):
        for pair in range(2):
            rows = filtered[pair * 384 : pair * 384 + 384, k * 256 : k * 256 + 256]
            filtered_t[k * 256 : k * 256 + 256, pair * 384 : pair * 384 + 384] = rows.T
    for i in range(4):
        make_band(band_back, i, True)

    own_modes.wait()
    whole_wait(mode_buf.at[pl.ds(0, 16 * (LAT - 1)), :], sem.at[8])
    group = lax.rem(lax.div(lax.broadcasted_iota(jnp.int32, (1024, 128), 0), 4), 4)
    modes = mode_buf[...].astype(F32)
    for g in range(4):
        kept = jnp.where(group == g, modes, 0.0).astype(BF)
        spec[:, g * 128 : g * 128 + 128] = jnp.dot(
            rep_t[...], kept, preferred_element_type=F32
        ).astype(BF)
    gains = gain_all[...]
    mixed[:, 0:256] = (
        gains * jnp.dot(spec[:, 0:256], mixing_ref[...], preferred_element_type=F32)
    ).astype(BF)
    scaled_s[...] = (gains * spec[:, 256:512].astype(F32)).astype(BF)
    mixed[:, 256:512] = lax.dot_general(
        scaled_s[...], mixing_ref[...], (((1,), (1,)), ((), ())), preferred_element_type=F32
    ).astype(BF)
    group = lax.rem(lax.div(lax.broadcasted_iota(jnp.int32, (512, 128), 0), 4), 4)
    rows = rep[pl.ds(pl.multiple_of(half * 512, 512), 512), :]
    packed = jnp.zeros((512, 128), F32)
    for g in range(4):
        sums = jnp.dot(rows, mixed[:, g * 128 : g * 128 + 128], preferred_element_type=F32)
        packed = jnp.where(group == g, sums, packed)
    back_src[...] = packed.astype(BF)

    def send_back(d, carry):
        to = lax.rem(slot + d, 32)
        src = back_src.at[tile(to), :]
        dst = cycle_buf.at[tile(slot), :]
        send(src, dst, sem.at[10], sem.at[11], (half * 32 + to, b))
        return carry

    lax.fori_loop(1, 32, send_back, 0)
    own_back = pltpu.make_async_copy(
        back_src.at[tile(slot), :], cycle_buf.at[tile(slot), :], sem.at[12]
    )
    own_back.start()

    degrees = pl.ds(pl.multiple_of((half * 4 + b) * 48, 16), 48)
    term = lax.dot_general(
        spec[degrees, 0:256],
        scaled_s[degrees, :],
        (((0,), (0,)), ((), ())),
        preferred_element_type=F32,
    )
    for h in range(2):
        terms[h, 1024:1280, :] = term[:, h * 128 : h * 128 + 128]

    own_back.wait()
    whole_wait(cycle_buf.at[pl.ds(0, 16 * 31), :], sem.at[11])
    cycle_wide[...] = cycle_buf[...].astype(F32)

    def cycle_rows(which, i):
        return jnp.concatenate(
            [cycle_wide[pl.ds(which * 8 + h * 4 + i, 32, stride=16), :] for h in range(2)], axis=1
        )

    for i in (0, 3, 1, 2):
        near_cycles[i + 1] = (cycle_rows(1, i) * cycle_weight_ref[i]).astype(BF)
    near_copies = [
        send(near_cycles.at[1], near_cycles.at[5], near_sem.at[0], near_sem.at[1], (north, b)),
        send(near_cycles.at[4], near_cycles.at[0], near_sem.at[2], near_sem.at[3], (south, b)),
    ]

    def make_grad(r):
        spatial = jnp.dot(wide_ref[b, 0], near_cycles[r], preferred_element_type=F32).astype(BF)
        return (cot_wide[r].astype(F32) + spatial.astype(F32)).astype(BF)

    whole_wait(rims_size(cot_wide), sem.at[6])
    for i in range(4):
        grad = make_grad(i + 1)
        grad_wide[i + 1] = grad
        grad_own[i * WIDTH : i * WIDTH + WIDTH, :] = grad[16 : 16 + WIDTH]
    for k in range(BASIS_COUNT):
        own = slice(k * 256, k * 256 + 256)
        term = jnp.dot(filtered_t[own, :], grad_own[...], preferred_element_type=F32)
        for h in range(2):
            terms[h, own, :] = term[:, h * 128 : h * 128 + 128]

    core_src[...] = terms[1 - core].astype(BF)
    core_copy = send(core_src, core_buf, sem.at[13], sem.at[14], (a, other_core))

    for i in range(4):
        fore_cycles[i] = cycle_rows(0, i).astype(BF)
    for i in range(4):
        spatial = jnp.dot(
            wide_ref[b, 1, 16 : 16 + WIDTH, :], fore_cycles[i], preferred_element_type=F32
        ).astype(BF)
        out_ref[i] = (hidden[i].astype(F32) + spatial.astype(F32)).astype(BF)

    core_copy.wait()
    plane_src[...] = (terms[core] + core_buf[...].astype(F32)).astype(BF)

    def piece(g):
        return pl.ds(pl.multiple_of(g * PIECE, 16), PIECE)

    def send_plane(d, carry):
        g = lax.rem(place + d, 16)
        send(
            plane_src.at[piece(g), :], plane_buf.at[place], sem.at[15], sem.at[16], plane_peer(g)
        )
        return carry

    lax.fori_loop(1, 16, send_plane, 0)
    own_piece = pltpu.make_async_copy(
        plane_src.at[piece(place), :], plane_buf.at[place], sem.at[17]
    )
    own_piece.start()

    for copy in near_copies:
        copy.wait()
    for r in (0, 5):
        grad_wide[r] = make_grad(r)

    def field_grad(i):
        total = grad_own[i * WIDTH : i * WIDTH + WIDTH, :].astype(F32)
        parts = []
        for block in range(2):
            sums = stencil(grad_wide, band_back, i, block)
            part = total[block * 96 : block * 96 + 96]
            for k in range(BASIS_COUNT):
                part = part + lax.dot_general(
                    sums[k * 96 : k * 96 + 96],
                    filter_ref[k * 256 : k * 256 + 256, :],
                    (((1,), (1,)), ((), ())),
                    preferred_element_type=F32,
                )
            parts.append(part)
        grad_ref[i] = jnp.concatenate(parts).astype(BF)

    field_grad(0)
    field_grad(1)

    own_piece.wait()
    whole_wait(plane_buf.at[pl.ds(0, 15)], sem.at[16])
    total = plane_buf[0].astype(F32)
    for g in range(1, 16):
        total = total + plane_buf[g].astype(F32)
    z_buf[z] = total.astype(BF)

    def send_z(d, carry):
        send(z_buf.at[z], z_buf.at[z], sem.at[18], sem.at[19], z_peer(lax.rem(z + d, 8)))
        return carry

    lax.fori_loop(1, 8, send_z, 0)
    field_grad(2)
    whole_wait(z_buf.at[pl.ds(0, 7)], sem.at[19])
    total = z_buf[0].astype(F32)
    for g in range(1, 8):
        total = total + z_buf[g].astype(F32)
    mine = whole_buf.at[core, piece(place), :]
    whole_buf[core, piece(place), :] = total.astype(BF)

    def send_piece(d, carry):
        send(mine, mine, sem.at[20], sem.at[21], plane_peer(lax.rem(place + d, 16)))
        return carry

    lax.fori_loop(1, 16, send_piece, 0)
    field_grad(3)
    whole_wait(whole_buf.at[core, pl.ds(0, 15 * PIECE), :], sem.at[21])
    whole_wait(whole_buf.at[core, pl.ds(0, 15 * PIECE), :], sem.at[20])
    last_copy = send(
        whole_buf.at[core], whole_buf.at[core], sem.at[22], sem.at[23], (a, other_core)
    )

    whole_wait(rims_size(field_wide), sem.at[0])
    whole_wait(table_buf.at[pl.ds(0, LAT - 1)], sem.at[2])
    whole_wait(rims_size(cot_wide), sem.at[5])
    whole_wait(mode_buf.at[pl.ds(0, 16 * (LAT - 1)), :], sem.at[7])
    whole_wait(cycle_buf.at[pl.ds(0, 16 * 31), :], sem.at[10])
    whole_wait(plane_buf.at[pl.ds(0, 15)], sem.at[15])
    whole_wait(z_buf.at[pl.ds(0, 7)], sem.at[18])
    last_copy.wait()

    grid_scale = (LATITUDES * LONGITUDES) ** (-0.5)
    for h in range(2):
        lanes = slice(h * 128, h * 128 + 128)
        grad_filter_ref[:, lanes] = whole_buf[h, 0:1024, :].astype(F32) * grid_scale
    columns = whole_buf[y_hi, 1024:1280, :].astype(F32) * (2 * ORDERS * DEGREES) ** (-0.5)
    grad_spectral_ref[...] = jnp.where(core == 0, columns[:, 0:64], columns[:, 64:128])


def block_call(taps, cycle_weight, field, cotangent, legendre, gain, mixing, filter_weight):
    pick, gain_pick = unpack_constants()
    wide, across = trig_tables()
    vmem = pl.BlockSpec(memory_space=pltpu.VMEM)
    smem = pl.BlockSpec(memory_space=pltpu.SMEM)
    dma = pltpu.SemaphoreType.DMA
    return pl.pallas_call(
        block_kernel,
        out_shape=(
            jax.ShapeDtypeStruct((4, WIDTH, 256), BF),
            jax.ShapeDtypeStruct((4, WIDTH, 256), BF),
            jax.ShapeDtypeStruct((1024, 256), F32),
            jax.ShapeDtypeStruct((256, 64), F32),
        ),
        in_specs=[smem] * 2 + [vmem] * 10,
        out_specs=(vmem,) * 4,
        scratch_shapes=[
            pltpu.VMEM((6, WIDE, 256), BF),
            pltpu.VMEM((6, WIDE, 256), BF),
            pltpu.VMEM((6, WIDE, 256), BF),
            pltpu.VMEM((4, 384, 384), BF),
            pltpu.VMEM((4, 384, 384), BF),
            pltpu.VMEM((768, 1024), BF),
            pltpu.VMEM((1024, 768), BF),
            pltpu.VMEM((4, WIDTH, 256), BF),
            pltpu.VMEM((768, 256), BF),
            pltpu.VMEM((2, 256, 128), F32),
            pltpu.VMEM((2, 256, 128), BF),
            pltpu.VMEM((2, 3, 256, 128), BF),
            pltpu.VMEM((3, 16, 128), BF),
            pltpu.VMEM((16, 32, 128), BF),
            pltpu.VMEM((LAT, 32, 128), BF),
            pltpu.VMEM((512, 128), BF),
            pltpu.VMEM((1024, 128), BF),
            pltpu.VMEM((1024, DEGREES), BF),
            pltpu.VMEM((DEGREES, 1024), BF),
            pltpu.VMEM((DEGREES, 256), F32),
            pltpu.VMEM((DEGREES, 512), BF),
            pltpu.VMEM((DEGREES, 256), BF),
            pltpu.VMEM((DEGREES, 512), BF),
            pltpu.VMEM((512, 128), BF),
            pltpu.VMEM((512, 128), BF),
            pltpu.VMEM((512, 128), F32),
            pltpu.VMEM((4, 32, 256), BF),
            pltpu.VMEM((6, 32, 256), BF),
            pltpu.VMEM((2, ROWS, 128), F32),
            pltpu.VMEM((ROWS, 128), BF),
            pltpu.VMEM((ROWS, 128), BF),
            pltpu.VMEM((ROWS, 128), BF),
            pltpu.VMEM((16, PIECE, 128), BF),
            pltpu.VMEM((8, PIECE, 128), BF),
            pltpu.VMEM((2, ROWS, 128), BF),
            dma((24,)),
            dma((3, 2, 3)),
            dma((4,)),
        ],
        compiler_params=pltpu.CompilerParams(
            collective_id=0, has_side_effects=True, vmem_limit_bytes=48 * 2**20
        ),
        name="block",
    )(
        taps,
        cycle_weight,
        field,
        cotangent,
        legendre,
        gain,
        mixing,
        filter_weight,
        jnp.asarray(pick, BF),
        jnp.asarray(gain_pick, BF),
        jnp.asarray(wide, BF),
        jnp.asarray(across, BF),
    )


def per_device(
    field,
    cotangent,
    legendre,
    cycle_weight,
    support_tap,
    support_basis,
    support_weight,
    filter_weight,
    spectral_weight,
    spectral_gain,
):
    lat, lon = lax.axis_index("lat"), lax.axis_index("lon")
    spots = lat * 4 - 1 + jnp.arange(6, dtype=jnp.int32)
    inside = (spots >= 0) & (spots < LATITUDES)
    code = support_tap * BASIS_COUNT + support_basis
    reach = jnp.clip(spots, 0, LATITUDES - 1)
    hit = code[reach][:, :, None] == jnp.arange(9 * BASIS_COUNT, dtype=jnp.int32)
    hit = hit & inside[:, None, None]
    taps = jnp.sum(jnp.where(hit, support_weight[reach][:, :, None], 0.0), axis=1)
    taps = taps.astype(BF).astype(F32)
    table = legendre.reshape(16, 3, 128, 4).transpose(0, 1, 3, 2).reshape(16, 12, 128)
    table = jnp.pad(table, ((0, 0), (0, 4), (0, 0)))
    at = jnp.arange(4, dtype=jnp.int32) == lon
    gain = jnp.where(at[None, :, None], spectral_gain[:, None, :], 0).reshape(6, 2, 128)
    gain = jnp.pad(gain.transpose(1, 0, 2).reshape(12, 128), ((0, 4), (0, 0)))
    output, grad_field, grad_filter, grad_spectral = block_call(
        taps,
        cycle_weight,
        field,
        cotangent,
        table,
        gain,
        spectral_weight,
        filter_weight.reshape(1024, 256),
    )
    return (output, grad_field, grad_filter.reshape(4, 256, 256), grad_spectral)


def solution(mesh):
    placed = (
        P("lat", "lon", None),
        P("lat", "lon", None),
        P(None, None, "lat"),
        P("lat"),
        P(),
        P(),
        P(),
        P(),
        P(),
        P("lat", "lon"),
    )
    return jax.shard_map(
        per_device,
        mesh=mesh,
        in_specs=placed,
        out_specs=(P("lat", "lon", None), P("lat", "lon", None), P(), P(None, "lon")),
        check_vma=False,
    )
```

time: 2070 us -> 91.5 us (0.04)
  waiting for transfers between devices: 1640 us -> 0 us
  blocking collectives: 137 us -> 0 us
  starting transfers between devices: 121 us -> 0 us
  local copies, waits for them, and re-layouts: 102 us -> 12.1 us
  Pallas kernels: 0 us -> 77.2 us
  matrix products: 36.1 us -> 0 us
    psum x2 -> x0, waiting for transfers between devices: 704 us -> none  [the longest x1 417 us: per_device(): grad_spectral = lax.psum(spectral_term, 'lat')]
    all_gather x2 -> x0, waiting for transfers between devices: 476 us -> none  [spectral_pass(): lax.all_gather(flat_mixed, 'lat', axis=0, tiled=True)]
    reduce_scatter x2 -> x0, waiting for transfers between devices: 442 us -> none  [spectral_pass(): lax.psum_scatter(jnp.einsum('mla,amx->lmx', degree_block, flat_modes, pre...]
    all_gather x2 -> x0, blocking collectives: 120 us -> none  [spectral_pass(): whole = lax.all_gather(local, 'lon', axis=3, tiled=True)]
    all_to_all x3 -> x0, starting transfers between devices: 106 us -> none  [the longest x2 99.8 us: spectral_pass(): lax.all_to_all(spatial, 'lon', split_axis=1, concat_axis=2, tiled=True)]
    pallas_call x0 -> x1, Pallas kernels: none -> 77.2 us  [block_call(): pl.pallas_call(block_kernel, out_shape=(jax.ShapeDtypeStruct((4, WIDTH, 2...]
    another operation x11 -> x0, local copies, waits for them, and re-layouts: 40.3 us -> none  [filter_rows(): jnp.stack([extended[north:north + count, east:east + width] for north in...]
    dot_general x25 -> x0, matrix products: 36.1 us -> none  [the longest x9 15.4 us: spread_back(): jnp.einsum('ak,ajkc->ajc', weights, values, preferred_element_type=jnp.fl...]
  transfers between devices with their start and end apart: 17 -> 0, of which waited for: 10 -> 0; matrix products, arithmetic and copies ran while one was open for 7% -> 0% of each run, Pallas kernels for 0% -> 0%
where the time goes in v1:
time: 91.5 us; the launch traced here: 91.1 us
  Pallas kernels  77.2 us (84%)
  local copies, waits for them, and re-layouts  12.1 us (13%)
  other arithmetic  0.99 us (1%)
    pallas_call x1, Pallas kernels, block_call(): pl.pallas_call(block_kernel, out_shape=(jax.ShapeDtypeStruct((4, WIDTH, 2...  77.2 us
    unnamed x26, local copies, waits for them, and re-layouts  10.5 us

profile of v1, /device:TPU:1, one launch (start us, length us, event | category | flops | bytes accessed | tf_op | source)
XLA Modules:
  0.0 91.1 jit_solution(1325350169482427512)
XLA Ops:
  0.6 0.0 copy-start.9
  0.7 0.0 copy-start.5
  0.7 0.1 broadcast_in_dim.48
  0.7 0.1 broadcast_in_dim.49
  0.9 0.5 copy-done.9
  1.3 0.1 broadcast_in_dim.52
  1.5 0.0 copy-start
  1.5 0.8 multiply_add_fusion
  2.3 0.8 copy.41
  3.1 0.0 copy-start.1
  3.2 0.1 copy.39
  3.3 0.6 gather_fusion
  3.9 0.8 copy.40
  4.7 0.6 gather_fusion.1
  5.3 0.1 select_reduce_fusion
  5.4 0.0 copy-start.8
  5.4 0.0 copy-done.5
  5.5 0.0 copy-done
  5.5 0.0 copy-done.1
  5.5 0.6 copy-done.8
  6.1 0.0 copy-start.2
  6.1 1.0 %copy-done.2 = bf16[4,192,256]{2,1,0:T(8,128)(2,1)S(1)} copy-done((bf16[4,192,256]{2,1,0:T(8,128)(2,1)S(1)}, bf16[4,192,256]{2,1,0:T(8,128)(2,1)}, u32[]{:S(2)}) %copy-start.2) | copy-done | bytes 393240
  7.1 0.0 copy-start.3
  7.1 1.0 %copy-done.3 = bf16[4,192,256]{2,1,0:T(8,128)(2,1)S(1)} copy-done((bf16[4,192,256]{2,1,0:T(8,128)(2,1)S(1)}, bf16[4,192,256]{2,1,0:T(8,128)(2,1)}, u32[]{:S(2)}) %copy-start.3) | copy-done | bytes 393240
  8.1 0.9 %copy-done.4 = bf16[3,128,256]{2,1,0:T(8,128)(2,1)S(1)} copy-done((bf16[3,128,256]{2,1,0:T(8,128)(2,1)S(1)}, bf16[3,128,256]{2,1,0:T(8,128)(2,1)}, u32[]{:S(2)}) %copy-start.4) | copy-done | bytes 196632
  9.0 0.9 copy-done.6
  9.9 0.8 copy-done.7
  10.7 77.2 %block.1 = (bf16[4,192,256]{2,1,0:T(8,128)(2,1)S(1)}, bf16[4,192,256]{2,1,0:T(8,128)(2,1)S(1)}, f32[1024,256]{1,0:T(8,128)S(1)}, f32[256,64]{1,0:T(8,128)S(1)}) custom-call(f32[6,36]{1,0:T(8,128)S(1)} %convert_element_type.16.tap_ref, f32[4]{0:T(128)S(1)} %copy-done.8, bf16[4,192,256]{2,1,0:T(8,128)(2,1)S(1)} %copy-done.2, ...), custom_call_target="tpu_custom_call" | custom-call | tf_op jit(solution)/shard_map/block/pallas_call | solution.py:518
  87.9 0.7 copy.45
  88.6 0.7 copy.49
  89.4 0.7 copy.50
  90.1 1.0 %copy.51 = f32[4,256,256]{2,1,0:T(8,128)} copy(f32[4,256,256]{2,1,0:T(8,128)S(1)} %bitcast.10) | data formatting | bytes 2097152
  (17 shorter events, 0.1 us)
Async XLA Ops:
  0.6 0.7 copy-start.9
  0.7 4.8 %copy-start.5 = (bf16[256,256]{1,0:T(8,128)(2,1)S(1)}, bf16[256,256]{1,0:T(8,128)(2,1)}, u32[]{:S(2)}) copy-start(bf16[256,256]{1,0:T(8,128)(2,1)} %mixing_ref.1) | copy-start | bytes 393220
  1.5 4.0 %copy-start = (bf16[4,256,256]{2,1,0:T(8,128)(2,1)S(1)}, bf16[4,256,256]{2,1,0:T(8,128)(2,1)}, u32[]{:S(2)}) copy-start(bf16[4,256,256]{2,1,0:T(8,128)(2,1)} %param.21) | copy-start | bytes 1572868
  3.1 2.3 %copy-start.1 = (bf16[4,2,224,32]{3,2,1,0:T(8,128)(2,1)S(1)}, bf16[4,2,224,32]{3,2,1,0:T(8,128)(2,1)}, u32[]{:S(2)}) copy-start(bf16[4,2,224,32]{3,2,1,0:T(8,128)(2,1)} %constant.38.clone.wide_ref) | copy-start | bytes 344068
  5.4 0.7 copy-start.8
  6.1 1.0 %copy-start.2 = (bf16[4,192,256]{2,1,0:T(8,128)(2,1)S(1)}, bf16[4,192,256]{2,1,0:T(8,128)(2,1)}, u32[]{:S(2)}) copy-start(bf16[4,192,256]{2,1,0:T(8,128)(2,1)} %field_ref.1) | copy-start | bytes 1179652
  7.1 1.0 %copy-start.3 = (bf16[4,192,256]{2,1,0:T(8,128)(2,1)S(1)}, bf16[4,192,256]{2,1,0:T(8,128)(2,1)}, u32[]{:S(2)}) copy-start(bf16[4,192,256]{2,1,0:T(8,128)(2,1)} %cot_ref.1) | copy-start | bytes 1179652
  8.1 0.9 %copy-start.4 = (bf16[3,128,256]{2,1,0:T(8,128)(2,1)S(1)}, bf16[3,128,256]{2,1,0:T(8,128)(2,1)}, u32[]{:S(2)}) copy-start(bf16[3,128,256]{2,1,0:T(8,128)(2,1)} %constant.36.clone.pick_ref) | copy-start | bytes 589828
  9.0 0.9 copy-start.6
  9.9 0.8 copy-start.7

commit v2 on v1

v2 whole, which is shorter than its diff:
```python
import math

import jax
import jax.numpy as jnp
import numpy as np
from jax import lax
from jax.experimental import pallas as pl
from jax.experimental.pallas import tpu as pltpu
from jax.sharding import PartitionSpec as P

LATITUDES = 256
LONGITUDES = 768
DEGREES = 384
ORDERS = 16
BASIS_COUNT = 4
LAT = 64
LON = 4
WIDTH = LONGITUDES // LON
WIDE = WIDTH + 32
ROWS = 1280
PIECE = 80
MESH = pl.DeviceIdType.MESH
BF = jnp.bfloat16
F32 = jnp.float32


def trig_tables():
    longitude = np.arange(LONGITUDES)
    order = np.arange(ORDERS)
    angle = (longitude[:, None] * order[None, :] % LONGITUDES) * (2.0 * math.pi / LONGITUDES)
    table = np.stack([np.cos(angle), np.sin(angle)], axis=2).reshape(LONGITUDES, 2 * ORDERS)
    both = np.stack([table * LONGITUDES ** (-0.5), table * (2 * ORDERS) ** (-0.5)])
    both = both.astype(np.float32)
    where = np.arange(LON)[:, None] * WIDTH + np.arange(-16, WIDTH + 16)[None, :]
    wide = both[:, where % LONGITUDES].transpose(1, 0, 2, 3)
    across = wide[:, :, 16 : 16 + WIDTH].transpose(0, 1, 3, 2)
    return wide, across


def whole_wait(ref, sem):
    pltpu.make_async_copy(ref, ref, sem).wait()


def unpack_constants():
    pick = np.zeros((3, 128, 256), np.float32)
    gain_pick = np.zeros((2, 48, 256), np.float32)
    for dev in range(8):
        for block in range(3):
            for group in range(4):
                for cycle in range(4):
                    pick[block, dev * 16 + group * 4 + cycle, dev * 32 + block * 4 + cycle] = 1.0
        for half in range(2):
            for degree in range(6):
                gain_pick[half, dev * 6 + degree, dev * 32 + 16 + half * 6 + degree] = 1.0
    return pick, gain_pick


def block_kernel(
    cycle_weight_ref,
    field_ref,
    cot_ref,
    legendre_ref,
    gain_ref,
    mixing_hbm,
    filter_hbm,
    pick_hbm,
    gain_pick_hbm,
    wide_hbm,
    across_hbm,
    support_tap_hbm,
    support_basis_hbm,
    support_weight_hbm,
    out_ref,
    grad_ref,
    sums_ref,
    mixing_ref,
    filter_ref,
    pick_ref,
    gain_pick_ref,
    wide_ref,
    across_ref,
    support_tap_ref,
    support_basis_ref,
    support_weight_ref,
    field_wide,
    cot_wide,
    grad_wide,
    band,
    band_back,
    filtered,
    filtered_t,
    hidden,
    grad_own,
    partial,
    part_buf,
    gain_wide,
    gain_src,
    gain_buf,
    table_src,
    table_buf,
    mode_buf,
    rep,
    rep_t,
    gain_all,
    spec,
    scaled_s,
    mixed,
    back_src,
    cycle_buf,
    cycle_wide,
    near_cycles,
    terms,
    core_src,
    core_buf,
    plane_src,
    plane_buf,
    z_buf,
    sem,
    lon_sem,
    near_sem,
    load_sem,
    sum_sem,
):
    a = lax.axis_index("lat")
    b = lax.axis_index("lon")
    x = lax.rem(a, 4)
    y_lo = lax.rem(lax.div(a, 4), 2)
    z = lax.div(a, 8)
    core = lax.rem(b, 2)
    y_hi = lax.div(b, 2)
    place = (y_hi * 2 + y_lo) * 4 + x
    other_core = y_hi * 2 + 1 - core
    north, south = lax.rem(a + LAT - 1, LAT), lax.rem(a + 1, LAT)
    west, east = lax.rem(b + LON - 1, LON), lax.rem(b + 1, LON)
    slot = z * 4 + x
    barrier = pltpu.get_barrier_semaphore()

    def plane_peer(g):
        py, px = lax.div(g, 4), lax.rem(g, 4)
        return (z * 8 + lax.rem(py, 2) * 4 + px, lax.div(py, 2) * 2 + core)

    def z_peer(g):
        return (g * 8 + y_lo * 4 + x, b)

    def greet(device):
        pl.semaphore_signal(barrier, inc=1, device_id=device, device_id_type=MESH)

    def row_peer(index):
        return lax.div(index, 4) * 8 + y_lo * 4 + lax.rem(index, 4)

    def greet_row(d, carry):
        greet((row_peer(lax.rem(slot + d, 32)), b))
        return carry

    def greet_source(d, carry):
        greet((lax.div(d, 4) * 8 + y_lo * 4 + b, lax.rem(d, 4)))
        return carry

    def greet_plane(d, carry):
        greet(plane_peer(lax.rem(place + d, 16)))
        return carry

    for d in range(1, LON):
        greet((a, lax.rem(b + d, LON)))
    for d in range(LON):
        greet((z * 8 + (1 - y_lo) * 4 + x, d))
    for lat in (north, south):
        greet((lat, b))
        for lon in (west, east):
            greet((lat, lon))
    lax.fori_loop(1, 16, greet_plane, 0)
    lax.fori_loop(1, 32, greet_row, 0)

    @pl.when(b == x)
    def greet_sources_but_me():
        def one(d, carry):
            index = lax.rem(z * 4 + b + d, 32)
            return greet_source(index, carry)

        lax.fori_loop(1, 32, one, 0)

    @pl.when(b != x)
    def greet_sources():
        lax.fori_loop(0, 32, greet_source, 0)

    def send(src, dst, send_sem, recv_sem, device):
        copy = pltpu.make_async_remote_copy(
            src_ref=src,
            dst_ref=dst,
            send_sem=send_sem,
            recv_sem=recv_sem,
            device_id=device,
            device_id_type=MESH,
        )
        copy.start()
        return copy

    inner, middle = pl.ds(1, 4), pl.ds(16, WIDTH)
    loads = [
        pltpu.make_async_copy(src, dst, load_sem.at[n])
        for n, (src, dst) in enumerate(
            (
                (field_ref, field_wide.at[inner, middle, :]),
                (cot_ref, cot_wide.at[inner, middle, :]),
                (across_hbm.at[b], across_ref),
                (support_tap_hbm, support_tap_ref),
                (support_basis_hbm, support_basis_ref),
                (support_weight_hbm, support_weight_ref),
                (filter_hbm, filter_ref),
                (pick_hbm, pick_ref),
                (gain_pick_hbm, gain_pick_ref),
                (mixing_hbm, mixing_ref),
                (wide_hbm.at[b], wide_ref),
            )
        )
    ]
    for load in loads:
        load.start()

    lane = lax.broadcasted_iota(jnp.int32, (6, 128), 1)
    own_gain = gain_ref[...].astype(F32)
    own_gain = jnp.concatenate([own_gain, own_gain], axis=1)
    own_gain = jnp.where(lax.div(lane, 64) == core, own_gain, 0.0)
    gain_wide[...] = jnp.zeros((16, 128), F32)
    for h in range(2):
        gain_wide[h * 6 : h * 6 + 6, :] = jnp.where(y_hi == h, own_gain, 0.0)
    gain_src[...] = gain_wide[...].astype(BF)

    def pack_partial(which, table, rows, scale):
        for i in range(4):
            sums = jnp.dot(across_ref[table], rows(i), preferred_element_type=F32)
            if scale:
                sums = sums * cycle_weight_ref[i]
            for h in range(2):
                partial[which, pl.ds(h * 4 + i, 32, stride=8), :] = sums[:, h * 128 : h * 128 + 128]

    def eight(index):
        return pl.ds(pl.multiple_of(index * 8, 8), 8)

    def send_partial(which, send_sem, recv_sem, own_sem):
        def remote(tr):
            src, dst = partial.at[which, eight(tr), :], part_buf.at[which, z, b]
            send(src, dst, send_sem, recv_sem, (row_peer(tr), x))

        def one(d, carry):
            remote(lax.rem(slot + d, 32))
            return carry

        @pl.when(b == x)
        def to_me():
            pltpu.make_async_copy(
                partial.at[which, eight(slot), :], part_buf.at[which, z, b], own_sem
            ).start()

        @pl.when(b != x)
        def to_peer():
            remote(slot)

        lax.fori_loop(1, 32, one, 0)

    def partial_size(which, count):
        return partial.at[which, pl.ds(0, 8 * count), :]

    def wait_partial(which, send_or_recv_sem, own_sem):
        @pl.when(b == x)
        def with_mine():
            if own_sem is not None:
                whole_wait(partial_size(which, 1), own_sem)
            whole_wait(partial_size(which, 31), send_or_recv_sem)

        @pl.when(b != x)
        def without():
            whole_wait(partial_size(which, 32), send_or_recv_sem)

    loads[0].wait()
    pl.semaphore_wait(barrier, 3 + 4 + 6 + 15 + 31 + 32 - jnp.where(b == x, 1, 0))

    def send_rims(wide, side_send, side_recv, lat_send, lat_recv):
        last, first = pl.ds(WIDTH, 16), pl.ds(16, 16)
        left, right = pl.ds(0, 16), pl.ds(WIDTH + 16, 16)
        top, bottom = wide.at[1], wide.at[4]
        send(wide.at[inner, last], wide.at[inner, left], side_send, side_recv, (a, east))
        send(wide.at[inner, first], wide.at[inner, right], side_send, side_recv, (a, west))
        send(bottom.at[middle], wide.at[0, middle], lat_send, lat_recv, (south, b))
        send(top.at[middle], wide.at[5, middle], lat_send, lat_recv, (north, b))
        send(bottom.at[last], wide.at[0, left], lat_send, lat_recv, (south, east))
        send(bottom.at[first], wide.at[0, right], lat_send, lat_recv, (south, west))
        send(top.at[last], wide.at[5, left], lat_send, lat_recv, (north, east))
        send(top.at[first], wide.at[5, right], lat_send, lat_recv, (north, west))

    def side_size(wide):
        return wide.at[pl.ds(0, 4), pl.ds(0, 32), :]

    def lat_size(wide):
        return wide.at[pl.ds(0, 2), :, :]

    def to_lon(src, buf, kind):
        return [
            send(
                src,
                buf.at[d - 1],
                lon_sem.at[kind, 0, d - 1],
                lon_sem.at[kind, 1, d - 1],
                (a, lax.rem(b + d, LON)),
            )
            for d in range(1, LON)
        ]

    send_rims(field_wide, sem.at[0], sem.at[1], sem.at[24], sem.at[25])
    gain_copies = to_lon(gain_src, gain_buf, 0)

    for copy in gain_copies:
        copy.wait()
    gain_row = gain_src[...].astype(F32)
    for d in range(LON - 1):
        gain_row = gain_row + gain_buf[d].astype(F32)
    gain_row = gain_row.astype(BF)
    for t in range(ORDERS):
        table_src[t, 0:16, :] = legendre_ref[t]
        table_src[t, 16:32, :] = gain_row

    def send_table(d, carry):
        to_z, to_x = lax.rem(z + d, 8), lax.rem(b + 1, 4)
        src = table_src.at[to_z * 2 + lax.div(to_x, 2)]
        dst = table_buf.at[z, y_lo, lax.div(x, 2), lax.rem(x, 2)]
        send(src, dst, sem.at[2], sem.at[3], (to_z * 8 + y_lo * 4 + to_x, x))
        return carry

    lax.fori_loop(0, 8, send_table, 0)
    loads[1].wait()
    loads[2].wait()
    pack_partial(1, 1, lambda i: cot_wide[i + 1, 16 : 16 + WIDTH, :], False)
    send_partial(1, sem.at[26], sem.at[27], sem.at[28])

    for load in loads[3:6]:
        load.wait()
    entry = lax.broadcasted_iota(jnp.int32, (18, 128), 1)
    place_of = lax.broadcasted_iota(jnp.int32, (18, LATITUDES), 1)
    code = (support_tap_ref[...] * BASIS_COUNT + support_basis_ref[...]).astype(F32)
    columns = []
    for r in range(6):
        here = place_of == a * 4 + r - 1
        own_code = jnp.sum(jnp.where(here, code, 0.0), axis=1, keepdims=True)
        own_weight = jnp.sum(
            jnp.where(here, support_weight_ref[...], 0.0), axis=1, keepdims=True
        )
        kept = jnp.where(own_code == entry.astype(F32), own_weight, 0.0)
        columns.append(jnp.sum(kept, axis=0, keepdims=True).astype(BF).astype(F32))

    diagonal = lax.broadcasted_iota(jnp.int32, (96, 128), 1)
    diagonal = diagonal - lax.broadcasted_iota(jnp.int32, (96, 128), 0) - 15
    inside_north = jnp.where(a == 0, 0.0, 1.0)
    inside_south = jnp.where(a == LAT - 1, 0.0, 1.0)

    def make_band(dst, i, adjoint):
        for p in range(3):
            for k in range(BASIS_COUNT):
                block = jnp.zeros((96, 128), F32)
                for q in range(3):
                    if adjoint:
                        column, at = columns[i + p], (8 - 3 * p - q) * BASIS_COUNT + k
                    else:
                        column, at = columns[i + 1], (3 * p + q) * BASIS_COUNT + k
                    value = column[:, at : at + 1]
                    if not adjoint:
                        if i == 0 and p == 0:
                            value = value * inside_north
                        if i == 3 and p == 2:
                            value = value * inside_south
                    block = jnp.where(diagonal == q, value, block)
                dst[i, k * 96 : k * 96 + 96, p * 128 : p * 128 + 128] = block.astype(BF)

    for i in range(4):
        make_band(band, i, False)

    def stencil(src, bands, i, block):
        near = jnp.concatenate([src[i + p, block * 96 : block * 96 + 128, :] for p in range(3)])
        return jnp.dot(bands[i], near, preferred_element_type=F32).astype(BF)

    whole_wait(table_buf.at[:, 0, 0, 0], sem.at[3])
    column_block = table_buf.at[:, y_lo, y_hi, core]
    for d in range(1, 4):
        y = lax.rem(y_hi * 2 + y_lo + d, 4)
        peer = (z * 8 + lax.rem(y, 2) * 4 + x, lax.div(y, 2) * 2 + core)
        send(column_block, column_block, sem.at[31], sem.at[32], peer)

    loads[6].wait()
    whole_wait(side_size(field_wide), sem.at[1])

    def filter_cycle(i):
        for block in range(2):
            sums = stencil(field_wide, band, i, block)
            first = i * WIDTH + block * 96
            for k in range(BASIS_COUNT):
                filtered[first : first + 96, k * 256 : k * 256 + 256] = sums[k * 96 : k * 96 + 96]
        own = slice(i * WIDTH, i * WIDTH + WIDTH)
        mix = jnp.dot(filtered[own, :], filter_ref[...], preferred_element_type=F32)
        own_field = field_wide[i + 1, 16 : 16 + WIDTH, :].astype(F32)
        hidden[i] = (own_field + mix).astype(BF)

    filter_cycle(1)
    filter_cycle(2)

    whole_wait(lat_size(field_wide), sem.at[25])
    filter_cycle(0)
    filter_cycle(3)
    pack_partial(0, 0, lambda i: hidden[i], True)
    send_partial(0, sem.at[7], sem.at[33], sem.at[9])

    whole_wait(table_buf.at[pl.ds(0, 6), 0], sem.at[32])
    core_table = table_buf.at[:, :, :, core]
    table_copy = send(core_table, core_table, sem.at[34], sem.at[35], (a, other_core))

    for k in range(BASIS_COUNT):
        for pair in range(2):
            rows = filtered[pair * 384 : pair * 384 + 384, k * 256 : k * 256 + 256]
            filtered_t[k * 256 : k * 256 + 256, pair * 384 : pair * 384 + 384] = rows.T
    for i in range(4):
        make_band(band_back, i, True)

    wait_partial(1, sem.at[27], sem.at[28])
    wait_partial(0, sem.at[33], sem.at[9])
    totals = []
    for which in range(2):
        total = part_buf[which, :, 0]
        for d in range(1, LON):
            total = total + part_buf[which, :, d]
        totals.append(total)
    mode_buf[:, y_lo, b] = jnp.concatenate(totals, axis=1).astype(BF)
    own_modes = mode_buf.at[:, y_lo, b]
    for d in range(1, 8):
        g = lax.rem(y_lo * 4 + b + d, 8)
        peer = (z * 8 + lax.div(g, 4) * 4 + x, lax.rem(g, 4))
        send(own_modes, own_modes, sem.at[36], sem.at[8], peer)

    def tile(index):
        return pl.ds(pl.multiple_of(index * 16, 16), 16)

    send_rims(cot_wide, sem.at[5], sem.at[6], sem.at[29], sem.at[30])

    for load in loads[7:]:
        load.wait()
    table_copy.wait()
    for chunk in range(8):
        packed = table_buf[chunk].reshape(256, 128)
        for block in range(3):
            rows = jnp.dot(pick_ref[block], packed, preferred_element_type=F32)
            lanes = slice(block * 128, block * 128 + 128)
            rep[chunk, :, :, lanes] = rows.astype(BF).reshape(2, 64, 128)
            rep_t[lanes, chunk * 128 : chunk * 128 + 128] = rows.T.astype(BF)
        for side in range(2):
            rows = jnp.dot(gain_pick_ref[side], packed, preferred_element_type=F32)
            gain_all[chunk * 48 : chunk * 48 + 48, side * 128 : side * 128 + 128] = rows

    whole_wait(mode_buf.at[pl.ds(0, 7)], sem.at[8])
    group = lax.rem(lax.div(lax.broadcasted_iota(jnp.int32, (1024, 128), 0), 4), 4)
    modes = mode_buf[...].reshape(1024, 128).astype(F32)
    for g in range(4):
        kept = jnp.where(group == g, modes, 0.0).astype(BF)
        spec[:, g * 128 : g * 128 + 128] = jnp.dot(
            rep_t[...], kept, preferred_element_type=F32
        ).astype(BF)
    gains = gain_all[...]
    mixed[:, 0:256] = (
        gains * jnp.dot(spec[:, 0:256], mixing_ref[...], preferred_element_type=F32)
    ).astype(BF)
    scaled_s[...] = (gains * spec[:, 256:512].astype(F32)).astype(BF)
    mixed[:, 256:512] = lax.dot_general(
        scaled_s[...], mixing_ref[...], (((1,), (1,)), ((), ())), preferred_element_type=F32
    ).astype(BF)
    group = lax.rem(lax.div(lax.broadcasted_iota(jnp.int32, (512, 128), 0), 4), 4)
    rows = rep[:, y_lo].reshape(512, DEGREES)
    packed = jnp.zeros((512, 128), F32)
    for g in range(4):
        sums = jnp.dot(rows, mixed[:, g * 128 : g * 128 + 128], preferred_element_type=F32)
        packed = jnp.where(group == g, sums, packed)
    back_src[...] = packed.astype(BF)

    def send_back(d, carry):
        to = lax.rem(slot + d, 32)
        src = back_src.at[tile(to), :]
        dst = cycle_buf.at[tile(slot), :]
        send(src, dst, sem.at[10], sem.at[11], (row_peer(to), b))
        return carry

    lax.fori_loop(1, 32, send_back, 0)
    own_back = pltpu.make_async_copy(
        back_src.at[tile(slot), :], cycle_buf.at[tile(slot), :], sem.at[12]
    )
    own_back.start()

    degrees = pl.ds(pl.multiple_of((y_lo * 4 + b) * 48, 16), 48)
    term = lax.dot_general(
        spec[degrees, 0:256],
        scaled_s[degrees, :],
        (((0,), (0,)), ((), ())),
        preferred_element_type=F32,
    )
    for h in range(2):
        terms[h, 1024:1280, :] = term[:, h * 128 : h * 128 + 128]

    parts = ((1024, 256), (0, 512), (512, 512))

    def part_rows(n):
        return pl.ds(parts[n][0], parts[n][1])

    def piece(n, g):
        size = parts[n][1] // 16
        return pl.ds(pl.multiple_of(parts[n][0] + g * size, 16), size)

    def plane_slots(n, count):
        size = parts[n][1] // 16
        return pl.ds(parts[n][0] // 16 * 15, count * size)

    def core_send(n):
        rows = part_rows(n)
        core_src[rows, :] = terms[1 - core, rows, :].astype(BF)
        return send(
            core_src.at[rows],
            core_buf.at[rows],
            sum_sem.at[n, 0],
            sum_sem.at[n, 1],
            (a, other_core),
        )

    def plane_send(n, core_copy):
        rows, size = part_rows(n), parts[n][1] // 16
        core_copy.wait()
        plane_src[rows, :] = (terms[core, rows, :] + core_buf[rows, :].astype(F32)).astype(BF)

        def one(d, carry):
            g = lax.rem(place + d, 16)
            slot_rows = pl.ds(
                pl.multiple_of(parts[n][0] // 16 * 15 + (d - 1) * size, 16), size
            )
            send(
                plane_src.at[piece(n, g)],
                plane_buf.at[slot_rows],
                sum_sem.at[n, 2],
                sum_sem.at[n, 3],
                plane_peer(g),
            )
            return carry

        lax.fori_loop(1, 16, one, 0)

    def z_rows(n):
        return pl.ds(parts[n][0] // 16, parts[n][1] // 16)

    def z_send(n):
        size = parts[n][1] // 16
        whole_wait(plane_buf.at[plane_slots(n, 15)], sum_sem.at[n, 3])
        total = plane_src[piece(n, place), :].astype(F32)
        for d in range(15):
            first = parts[n][0] // 16 * 15 + d * size
            total = total + plane_buf[first : first + size, :].astype(F32)
        z_buf[z, z_rows(n), :] = total.astype(BF)
        mine = z_buf.at[z, z_rows(n)]

        def one(d, carry):
            send(mine, mine, sum_sem.at[n, 4], sum_sem.at[n, 5], z_peer(lax.rem(z + d, 8)))
            return carry

        lax.fori_loop(1, 8, one, 0)

    def z_size(n):
        return z_buf.at[pl.ds(0, 7), z_rows(n)]

    def gather_send(n):
        whole_wait(z_size(n), sum_sem.at[n, 5])
        total = z_buf[0, z_rows(n), :].astype(F32)
        for g in range(1, 8):
            total = total + z_buf[g, z_rows(n), :].astype(F32)
        sums_ref[core, piece(n, place), :] = total.astype(BF)
        mine = sums_ref.at[core, piece(n, place)]

        def one(d, carry):
            send(
                mine,
                mine,
                sum_sem.at[n, 6],
                sum_sem.at[n, 7],
                plane_peer(lax.rem(place + d, 16)),
            )
            return carry

        lax.fori_loop(1, 16, one, 0)

    def last_send(n):
        whole_wait(plane_buf.at[plane_slots(n, 15)], sum_sem.at[n, 7])
        half_sums = sums_ref.at[core, part_rows(n)]
        return send(half_sums, half_sums, sum_sem.at[n, 8], sum_sem.at[n, 9], (a, other_core))

    spectral_copy = core_send(0)
    plane_send(0, spectral_copy)

    own_back.wait()
    whole_wait(cycle_buf.at[pl.ds(0, 16 * 31), :], sem.at[11])
    cycle_wide[...] = cycle_buf[...].astype(F32)

    def cycle_rows(which, i):
        return jnp.concatenate(
            [cycle_wide[pl.ds(which * 8 + h * 4 + i, 32, stride=16), :] for h in range(2)], axis=1
        )

    for i in (0, 3, 1, 2):
        near_cycles[i + 1] = (cycle_rows(1, i) * cycle_weight_ref[i]).astype(BF)
    near_copies = [
        send(near_cycles.at[1], near_cycles.at[5], near_sem.at[0], near_sem.at[1], (north, b)),
        send(near_cycles.at[4], near_cycles.at[0], near_sem.at[2], near_sem.at[3], (south, b)),
    ]

    def make_grad(r):
        spatial = jnp.dot(wide_ref[0], near_cycles[r], preferred_element_type=F32).astype(BF)
        return (cot_wide[r].astype(F32) + spatial.astype(F32)).astype(BF)

    whole_wait(side_size(cot_wide), sem.at[6])
    whole_wait(lat_size(cot_wide), sem.at[30])
    for i in range(4):
        grad = make_grad(i + 1)
        grad_wide[i + 1] = grad
        grad_own[i * WIDTH : i * WIDTH + WIDTH, :] = grad[16 : 16 + WIDTH]
    def filter_terms(k):
        own = slice(k * 256, k * 256 + 256)
        term = jnp.dot(filtered_t[own, :], grad_own[...], preferred_element_type=F32)
        for h in range(2):
            terms[h, own, :] = term[:, h * 128 : h * 128 + 128]

    filter_terms(0)
    filter_terms(1)
    first_copy = core_send(1)
    filter_terms(2)
    filter_terms(3)
    second_copy = core_send(2)
    z_send(0)
    plane_send(1, first_copy)

    def finish_output(i):
        fore = cycle_rows(0, i).astype(BF)
        spatial = jnp.dot(wide_ref[1, 16 : 16 + WIDTH, :], fore, preferred_element_type=F32)
        out_ref[i] = (hidden[i].astype(F32) + spatial.astype(BF).astype(F32)).astype(BF)

    finish_output(0)
    plane_send(2, second_copy)
    finish_output(1)
    gather_send(0)
    finish_output(2)
    finish_output(3)
    for copy in near_copies:
        copy.wait()
    for r in (0, 5):
        grad_wide[r] = make_grad(r)

    def field_grad(i):
        total = grad_own[i * WIDTH : i * WIDTH + WIDTH, :].astype(F32)
        done = []
        for block in range(2):
            sums = stencil(grad_wide, band_back, i, block)
            part = total[block * 96 : block * 96 + 96]
            for k in range(BASIS_COUNT):
                part = part + lax.dot_general(
                    sums[k * 96 : k * 96 + 96],
                    filter_ref[k * 256 : k * 256 + 256, :],
                    (((1,), (1,)), ((), ())),
                    preferred_element_type=F32,
                )
            done.append(part)
        grad_ref[i] = jnp.concatenate(done).astype(BF)

    z_send(1)
    field_grad(0)
    z_send(2)
    field_grad(1)
    last_copies = [last_send(0)]
    gather_send(1)
    field_grad(2)
    gather_send(2)
    field_grad(3)
    last_copies.append(last_send(1))
    last_copies.append(last_send(2))

    whole_wait(side_size(field_wide), sem.at[0])
    whole_wait(lat_size(field_wide), sem.at[24])
    whole_wait(side_size(cot_wide), sem.at[5])
    whole_wait(lat_size(cot_wide), sem.at[29])
    wait_partial(1, sem.at[26], None)
    wait_partial(0, sem.at[7], None)
    whole_wait(table_buf.at[:, 0, 0, 0], sem.at[2])
    whole_wait(table_buf.at[pl.ds(0, 6), 0], sem.at[31])
    whole_wait(mode_buf.at[pl.ds(0, 7)], sem.at[36])
    whole_wait(cycle_buf.at[pl.ds(0, 16 * 31), :], sem.at[10])
    for n in range(3):
        whole_wait(plane_buf.at[plane_slots(n, 15)], sum_sem.at[n, 2])
        whole_wait(z_size(n), sum_sem.at[n, 4])
        whole_wait(plane_buf.at[plane_slots(n, 15)], sum_sem.at[n, 6])
    for copy in last_copies:
        copy.wait()


def finish_kernel(sums_hbm, out_hbm, grad_hbm, out_ref, grad_ref, filter_ref, spectral_ref, *scratch):
    sums_ref, filter_vmem, spectral_vmem, out_vmem, grad_vmem, sem = scratch
    b = lax.axis_index("lon")
    copies = [
        pltpu.make_async_copy(sums_hbm, sums_ref, sem.at[0]),
        pltpu.make_async_copy(out_hbm, out_vmem, sem.at[1]),
        pltpu.make_async_copy(grad_hbm, grad_vmem, sem.at[2]),
    ]
    for copy in copies:
        copy.start()
    copies[0].wait()
    grid_scale = (LATITUDES * LONGITUDES) ** (-0.5)
    for k in range(BASIS_COUNT):
        for h in range(2):
            rows, lanes = slice(k * 256, k * 256 + 256), slice(h * 128, h * 128 + 128)
            filter_vmem[rows, lanes] = sums_ref[h, rows, :].astype(F32) * grid_scale
        rows = pl.ds(k * 256, 256)
        copies.append(
            pltpu.make_async_copy(filter_vmem.at[rows], filter_ref.at[rows], sem.at[3 + k])
        )
        copies[-1].start()
    columns = sums_ref[lax.div(b, 2), 1024:1280, :].astype(F32)
    columns = columns * (2 * ORDERS * DEGREES) ** (-0.5)
    spectral_vmem[...] = jnp.where(
        lax.rem(b, 2) == 0, columns[:, 0:64], columns[:, 64:128]
    ).T
    copies.append(pltpu.make_async_copy(spectral_vmem, spectral_ref, sem.at[7]))
    copies[-1].start()
    for n, (staged, target) in enumerate(((out_vmem, out_ref), (grad_vmem, grad_ref))):
        copies[1 + n].wait()
        copies.append(pltpu.make_async_copy(staged, target, sem.at[8 + n]))
        copies[-1].start()
    for copy in copies[3:]:
        copy.wait()


def finish_call(sums, out, grad):
    anywhere = pl.BlockSpec(memory_space=pl.ANY)
    return pl.pallas_call(
        finish_kernel,
        out_shape=(
            jax.ShapeDtypeStruct((4, WIDTH, 256), BF),
            jax.ShapeDtypeStruct((4, WIDTH, 256), BF),
            jax.ShapeDtypeStruct((1024, 256), F32),
            jax.ShapeDtypeStruct((64, 256), F32),
        ),
        in_specs=[anywhere] * 3,
        out_specs=(anywhere,) * 4,
        scratch_shapes=[
            pltpu.VMEM((2, ROWS, 128), BF),
            pltpu.VMEM((1024, 256), F32),
            pltpu.VMEM((64, 256), F32),
            pltpu.VMEM((4, WIDTH, 256), BF),
            pltpu.VMEM((4, WIDTH, 256), BF),
            pltpu.SemaphoreType.DMA((10,)),
        ],
        compiler_params=pltpu.CompilerParams(vmem_limit_bytes=60 * 2**20),
        name="finish",
    )(sums, out, grad)


def block_call(cycle_weight, field, cotangent, legendre, gain, mixing, filter_weight, support):
    pick, gain_pick = unpack_constants()
    wide, across = trig_tables()
    vmem = pl.BlockSpec(memory_space=pltpu.VMEM)
    smem = pl.BlockSpec(memory_space=pltpu.SMEM)
    anywhere = pl.BlockSpec(memory_space=pl.ANY)
    dma = pltpu.SemaphoreType.DMA
    return pl.pallas_call(
        block_kernel,
        out_shape=(
            jax.ShapeDtypeStruct((4, WIDTH, 256), BF),
            jax.ShapeDtypeStruct((4, WIDTH, 256), BF),
            jax.ShapeDtypeStruct((2, ROWS, 128), BF),
        ),
        in_specs=[smem, anywhere, anywhere, vmem, vmem] + [anywhere] * 9,
        out_specs=(vmem,) * 3,
        scratch_shapes=[
            pltpu.VMEM((256, 256), BF),
            pltpu.VMEM((1024, 256), BF),
            pltpu.VMEM((3, 128, 256), BF),
            pltpu.VMEM((2, 48, 256), BF),
            pltpu.VMEM((2, WIDE, 32), BF),
            pltpu.VMEM((2, 32, WIDTH), BF),
            pltpu.VMEM((18, LATITUDES), jnp.int32),
            pltpu.VMEM((18, LATITUDES), jnp.int32),
            pltpu.VMEM((18, LATITUDES), F32),
            pltpu.VMEM((6, WIDE, 256), BF),
            pltpu.VMEM((6, WIDE, 256), BF),
            pltpu.VMEM((6, WIDE, 256), BF),
            pltpu.VMEM((4, 384, 384), BF),
            pltpu.VMEM((4, 384, 384), BF),
            pltpu.VMEM((768, 1024), BF),
            pltpu.VMEM((1024, 768), BF),
            pltpu.VMEM((4, WIDTH, 256), BF),
            pltpu.VMEM((768, 256), BF),
            pltpu.VMEM((2, 256, 128), F32),
            pltpu.VMEM((2, 8, LON, 8, 128), F32),
            pltpu.VMEM((16, 128), F32),
            pltpu.VMEM((16, 128), BF),
            pltpu.VMEM((3, 16, 128), BF),
            pltpu.VMEM((16, 32, 128), BF),
            pltpu.VMEM((8, 2, 2, 2, 32, 128), BF),
            pltpu.VMEM((8, 2, 4, 16, 128), BF),
            pltpu.VMEM((8, 2, 64, DEGREES), BF),
            pltpu.VMEM((DEGREES, 1024), BF),
            pltpu.VMEM((DEGREES, 256), F32),
            pltpu.VMEM((DEGREES, 512), BF),
            pltpu.VMEM((DEGREES, 256), BF),
            pltpu.VMEM((DEGREES, 512), BF),
            pltpu.VMEM((512, 128), BF),
            pltpu.VMEM((512, 128), BF),
            pltpu.VMEM((512, 128), F32),
            pltpu.VMEM((6, 32, 256), BF),
            pltpu.VMEM((2, ROWS, 128), F32),
            pltpu.VMEM((ROWS, 128), BF),
            pltpu.VMEM((ROWS, 128), BF),
            pltpu.VMEM((ROWS, 128), BF),
            pltpu.VMEM((15 * PIECE, 128), BF),
            pltpu.VMEM((8, PIECE, 128), BF),
            dma((37,)),
            dma((1, 2, 3)),
            dma((4,)),
            dma((11,)),
            dma((3, 10)),
        ],
        compiler_params=pltpu.CompilerParams(
            collective_id=0, has_side_effects=True, vmem_limit_bytes=60 * 2**20
        ),
        name="block",
    )(
        cycle_weight,
        field,
        cotangent,
        legendre,
        gain,
        mixing,
        filter_weight,
        jnp.asarray(pick, BF),
        jnp.asarray(gain_pick, BF),
        jnp.asarray(wide, BF),
        jnp.asarray(across, BF),
        *support,
    )


def per_device(
    field,
    cotangent,
    legendre,
    cycle_weight,
    support_tap,
    support_basis,
    support_weight,
    filter_weight,
    spectral_weight,
    spectral_gain,
):
    table = legendre.reshape(16, 3, 128, 4).transpose(0, 1, 3, 2).reshape(16, 12, 128)
    table = jnp.pad(table, ((0, 0), (0, 4), (0, 0)))
    output, grad_field, sums = block_call(
        cycle_weight,
        field,
        cotangent,
        table,
        spectral_gain,
        spectral_weight,
        filter_weight.reshape(1024, 256),
        (support_tap.T, support_basis.T, support_weight.T),
    )
    output, grad_field, grad_filter, grad_spectral = finish_call(sums, output, grad_field)
    return (output, grad_field, grad_filter.reshape(4, 256, 256), grad_spectral.T)


def solution(mesh):
    placed = (
        P("lat", "lon", None),
        P("lat", "lon", None),
        P(None, None, "lat"),
        P("lat"),
        P(),
        P(),
        P(),
        P(),
        P(),
        P("lat", "lon"),
    )
    return jax.shard_map(
        per_device,
        mesh=mesh,
        in_specs=placed,
        out_specs=(P("lat", "lon", None), P("lat", "lon", None), P(), P(None, "lon")),
        check_vma=False,
    )
```

time: 91.5 us -> 81.1 us (0.89)
  local copies, waits for them, and re-layouts: 12.1 us -> 1.5 us
  Pallas kernels: 77.2 us -> 78.7 us
  other arithmetic: 0.99 us -> 0 us
    unnamed x26 -> x1, local copies, waits for them, and re-layouts: 10.5 us -> 0.81 us
    pallas_call x0 -> x1, Pallas kernels: none -> 2.52 us  [finish_call(): pl.pallas_call(finish_kernel, out_shape=(jax.ShapeDtypeStruct((4, WIDTH,...]
    gather x2 -> x0, local copies, waits for them, and re-layouts: 1.11 us -> none  [the longest x1 0.55 us: per_device(): code[reach][:, :, None] == jnp.arange(9 * BASIS_COUNT, dtype=jnp.int32)]
    pallas_call x1, Pallas kernels: 77.2 us -> 76.2 us  [block_call(): pl.pallas_call(block_kernel, out_shape=(jax.ShapeDtypeStruct((4, WIDTH, 2...]
where the time goes in v2:
time: 81.1 us; the launch traced here: 80.8 us
  Pallas kernels  78.7 us (97%)
  local copies, waits for them, and re-layouts  1.5 us (2%)
    pallas_call x1, Pallas kernels, block_call(): pl.pallas_call(block_kernel, out_shape=(jax.ShapeDtypeStruct((4, WIDTH, 2...  76.2 us
    pallas_call x1, Pallas kernels, finish_call(): pl.pallas_call(finish_kernel, out_shape=(jax.ShapeDtypeStruct((4, WIDTH,...  2.52 us

profile of v2, /device:TPU:1, one launch (start us, length us, event | category | flops | bytes accessed | tf_op | source)
XLA Modules:
  0.0 80.8 jit_solution(1281185951757976227)
XLA Ops:
  0.6 0.8 copy.19
  1.5 0.6 pad.4.legendre_ref
  2.1 76.2 %block.1 = (bf16[4,192,256]{2,1,0:T(8,128)(2,1)}, bf16[4,192,256]{2,1,0:T(8,128)(2,1)}, bf16[2,1280,128]{2,1,0:T(8,128)(2,1)}) custom-call(f32[4]{0:T(128)} %cycle_weight_ref.1, bf16[4,192,256]{2,1,0:T(8,128)(2,1)} %field_ref.1, bf16[4,192,256]{2,1,0:T(8,128)(2,1)} %cot_ref.1, bf16[16,16,128]{2,1,0:T(8,128)(2,1)} %pad.4.legendre_ref, ...), custom_call_target="tpu_custom_call" | custom-call | tf_op jit(solution)/shard_map/block/pallas_call | solution.py:768
  78.3 2.5 %finish.1 = (bf16[4,192,256]{2,1,0:T(8,128)(2,1)}, bf16[4,192,256]{2,1,0:T(8,128)(2,1)}, f32[1024,256]{1,0:T(8,128)}, f32[64,256]{1,0:T(8,128)}) custom-call(bf16[2,1280,128]{2,1,0:T(8,128)(2,1)} %get-tuple-element.11.sums_hbm, bf16[4,192,256]{2,1,0:T(8,128)(2,1)} %get-tuple-element.12.out_hbm, bf16[4,192,256]{2,1,0:T(8,128)(2,1)} %get-tuple-element.13.grad_hbm), custom_call_target="tpu_custom_call" | custom-call | tf_op jit(solution)/shard_map/finish/pallas_call | solution.py:738
  (3 shorter events, 0.1 us)

commit v3 on v2

--- a/solution.py
+++ b/solution.py
@@ -272,7 +272,6 @@
         def without():
             whole_wait(partial_size(which, 32), send_or_recv_sem)
 
-    loads[0].wait()
     pl.semaphore_wait(barrier, 3 + 4 + 6 + 15 + 31 + 32 - jnp.where(b == x, 1, 0))
 
     def send_rims(wide, side_send, side_recv, lat_send, lat_recv):
@@ -306,8 +305,12 @@
             for d in range(1, LON)
         ]
 
+    gain_copies = to_lon(gain_src, gain_buf, 0)
+    loads[0].wait()
     send_rims(field_wide, sem.at[0], sem.at[1], sem.at[24], sem.at[25])
-    gain_copies = to_lon(gain_src, gain_buf, 0)
+    loads[1].wait()
+    loads[2].wait()
+    pack_partial(1, 1, lambda i: cot_wide[i + 1, 16 : 16 + WIDTH, :], False)
 
     for copy in gain_copies:
         copy.wait()
@@ -327,9 +330,6 @@
         return carry
 
     lax.fori_loop(0, 8, send_table, 0)
-    loads[1].wait()
-    loads[2].wait()
-    pack_partial(1, 1, lambda i: cot_wide[i + 1, 16 : 16 + WIDTH, :], False)
     send_partial(1, sem.at[26], sem.at[27], sem.at[28])
 
     for load in loads[3:6]:
@@ -384,6 +384,23 @@
         peer = (z * 8 + lax.rem(y, 2) * 4 + x, lax.div(y, 2) * 2 + core)
         send(column_block, column_block, sem.at[31], sem.at[32], peer)
 
+    def gather_modes(which, send_sem, recv_sem):
+        total = part_buf[which, :, 0]
+        for d in range(1, LON):
+            total = total + part_buf[which, :, d]
+        halves = [total, jnp.zeros_like(total)]
+        if which == 1:
+            halves.reverse()
+        mode_buf[which, :, y_lo, b] = jnp.concatenate(halves, axis=1).astype(BF)
+        own_modes = mode_buf.at[which, :, y_lo, b]
+        for d in range(1, 8):
+            g = lax.rem(y_lo * 4 + b + d, 8)
+            peer = (z * 8 + lax.div(g, 4) * 4 + x, lax.rem(g, 4))
+            send(own_modes, own_modes, send_sem, recv_sem, peer)
+
+    wait_partial(1, sem.at[27], sem.at[28])
+    gather_modes(1, sem.at[36], sem.at[8])
+
     loads[6].wait()
     whole_wait(side_size(field_wide), sem.at[1])
 
@@ -404,37 +421,12 @@
     whole_wait(lat_size(field_wide), sem.at[25])
     filter_cycle(0)
     filter_cycle(3)
-    pack_partial(0, 0, lambda i: hidden[i], True)
-    send_partial(0, sem.at[7], sem.at[33], sem.at[9])
-
     whole_wait(table_buf.at[pl.ds(0, 6), 0], sem.at[32])
     core_table = table_buf.at[:, :, :, core]
     table_copy = send(core_table, core_table, sem.at[34], sem.at[35], (a, other_core))
-
-    for k in range(BASIS_COUNT):
-        for pair in range(2):
-            rows = filtered[pair * 384 : pair * 384 + 384, k * 256 : k * 256 + 256]
-            filtered_t[k * 256 : k * 256 + 256, pair * 384 : pair * 384 + 384] = rows.T
-    for i in range(4):
-        make_band(band_back, i, True)
-
-    wait_partial(1, sem.at[27], sem.at[28])
-    wait_partial(0, sem.at[33], sem.at[9])
-    totals = []
-    for which in range(2):
-        total = part_buf[which, :, 0]
-        for d in range(1, LON):
-            total = total + part_buf[which, :, d]
-        totals.append(total)
-    mode_buf[:, y_lo, b] = jnp.concatenate(totals, axis=1).astype(BF)
-    own_modes = mode_buf.at[:, y_lo, b]
-    for d in range(1, 8):
-        g = lax.rem(y_lo * 4 + b + d, 8)
-        peer = (z * 8 + lax.div(g, 4) * 4 + x, lax.rem(g, 4))
-        send(own_modes, own_modes, sem.at[36], sem.at[8], peer)
-
-    def tile(index):
-        return pl.ds(pl.multiple_of(index * 16, 16), 16)
+    pack_partial(0, 0, lambda i: hidden[i], True)
+    send_partial(0, sem.at[7], sem.at[33], sem.at[9])
+
 
     send_rims(cot_wide, sem.at[5], sem.at[6], sem.at[29], sem.at[30])
 
@@ -452,52 +444,66 @@
             rows = jnp.dot(gain_pick_ref[side], packed, preferred_element_type=F32)
             gain_all[chunk * 48 : chunk * 48 + 48, side * 128 : side * 128 + 128] = rows
 
-    whole_wait(mode_buf.at[pl.ds(0, 7)], sem.at[8])
-    group = lax.rem(lax.div(lax.broadcasted_iota(jnp.int32, (1024, 128), 0), 4), 4)
-    modes = mode_buf[...].reshape(1024, 128).astype(F32)
-    for g in range(4):
-        kept = jnp.where(group == g, modes, 0.0).astype(BF)
-        spec[:, g * 128 : g * 128 + 128] = jnp.dot(
-            rep_t[...], kept, preferred_element_type=F32
-        ).astype(BF)
-    gains = gain_all[...]
-    mixed[:, 0:256] = (
-        gains * jnp.dot(spec[:, 0:256], mixing_ref[...], preferred_element_type=F32)
-    ).astype(BF)
-    scaled_s[...] = (gains * spec[:, 256:512].astype(F32)).astype(BF)
-    mixed[:, 256:512] = lax.dot_general(
-        scaled_s[...], mixing_ref[...], (((1,), (1,)), ((), ())), preferred_element_type=F32
-    ).astype(BF)
-    group = lax.rem(lax.div(lax.broadcasted_iota(jnp.int32, (512, 128), 0), 4), 4)
-    rows = rep[:, y_lo].reshape(512, DEGREES)
-    packed = jnp.zeros((512, 128), F32)
-    for g in range(4):
-        sums = jnp.dot(rows, mixed[:, g * 128 : g * 128 + 128], preferred_element_type=F32)
-        packed = jnp.where(group == g, sums, packed)
-    back_src[...] = packed.astype(BF)
-
-    def send_back(d, carry):
-        to = lax.rem(slot + d, 32)
-        src = back_src.at[tile(to), :]
-        dst = cycle_buf.at[tile(slot), :]
-        send(src, dst, sem.at[10], sem.at[11], (row_peer(to), b))
-        return carry
-
-    lax.fori_loop(1, 32, send_back, 0)
-    own_back = pltpu.make_async_copy(
-        back_src.at[tile(slot), :], cycle_buf.at[tile(slot), :], sem.at[12]
-    )
-    own_back.start()
-
-    degrees = pl.ds(pl.multiple_of((y_lo * 4 + b) * 48, 16), 48)
-    term = lax.dot_general(
-        spec[degrees, 0:256],
-        scaled_s[degrees, :],
-        (((0,), (0,)), ((), ())),
-        preferred_element_type=F32,
-    )
-    for h in range(2):
-        terms[h, 1024:1280, :] = term[:, h * 128 : h * 128 + 128]
+    def tile(index):
+        return pl.ds(pl.multiple_of(index * 16, 16), 16)
+
+    def own_order(which, mode_recv, back_send, back_recv, own_sem):
+        whole_wait(mode_buf.at[which, pl.ds(0, 7)], mode_recv)
+        groups = (2 * which, 2 * which + 1)
+        group = lax.rem(lax.div(lax.broadcasted_iota(jnp.int32, (1024, 128), 0), 4), 4)
+        modes = mode_buf[which].reshape(1024, 128).astype(F32)
+        for g in groups:
+            kept = jnp.where(group == g, modes, 0.0).astype(BF)
+            spec[:, g * 128 : g * 128 + 128] = jnp.dot(
+                rep_t[...], kept, preferred_element_type=F32
+            ).astype(BF)
+        gains = gain_all[...]
+        if which == 0:
+            mix = jnp.dot(spec[:, 0:256], mixing_ref[...], preferred_element_type=F32)
+            mixed[:, 0:256] = (gains * mix).astype(BF)
+        else:
+            scaled_s[...] = (gains * spec[:, 256:512].astype(F32)).astype(BF)
+            mixed[:, 256:512] = lax.dot_general(
+                scaled_s[...], mixing_ref[...], (((1,), (1,)), ((), ())), preferred_element_type=F32
+            ).astype(BF)
+        group = lax.rem(lax.div(lax.broadcasted_iota(jnp.int32, (512, 128), 0), 4), 4)
+        rows = rep[:, y_lo].reshape(512, DEGREES)
+        packed = jnp.zeros((512, 128), F32)
+        for g in groups:
+            sums = jnp.dot(rows, mixed[:, g * 128 : g * 128 + 128], preferred_element_type=F32)
+            packed = jnp.where(group == g, sums, packed)
+        back_src[which] = packed.astype(BF)
+
+        def send_back(d, carry):
+            to = lax.rem(slot + d, 32)
+            src = back_src.at[which, tile(to), :]
+            dst = cycle_buf.at[which, tile(slot), :]
+            send(src, dst, back_send, back_recv, (row_peer(to), b))
+            return carry
+
+        lax.fori_loop(1, 32, send_back, 0)
+        own_back = pltpu.make_async_copy(
+            back_src.at[which, tile(slot), :], cycle_buf.at[which, tile(slot), :], own_sem
+        )
+        own_back.start()
+        return own_back
+
+    def wait_back(which, own_back, back_recv):
+        own_back.wait()
+        whole_wait(cycle_buf.at[which, pl.ds(0, 16 * 31), :], back_recv)
+        cycle_wide[which] = cycle_buf[which].astype(F32)
+
+    back_own = own_order(1, sem.at[8], sem.at[10], sem.at[11], sem.at[12])
+
+    for k in range(BASIS_COUNT):
+        for pair in range(2):
+            rows = filtered[pair * 384 : pair * 384 + 384, k * 256 : k * 256 + 256]
+            filtered_t[k * 256 : k * 256 + 256, pair * 384 : pair * 384 + 384] = rows.T
+    for i in range(4):
+        make_band(band_back, i, True)
+
+    wait_partial(0, sem.at[33], sem.at[9])
+    gather_modes(0, sem.at[37], sem.at[38])
 
     parts = ((1024, 256), (0, 512), (512, 512))
 
@@ -591,16 +597,11 @@
         half_sums = sums_ref.at[core, part_rows(n)]
         return send(half_sums, half_sums, sum_sem.at[n, 8], sum_sem.at[n, 9], (a, other_core))
 
-    spectral_copy = core_send(0)
-    plane_send(0, spectral_copy)
-
-    own_back.wait()
-    whole_wait(cycle_buf.at[pl.ds(0, 16 * 31), :], sem.at[11])
-    cycle_wide[...] = cycle_buf[...].astype(F32)
+    wait_back(1, back_own, sem.at[11])
 
     def cycle_rows(which, i):
         return jnp.concatenate(
-            [cycle_wide[pl.ds(which * 8 + h * 4 + i, 32, stride=16), :] for h in range(2)], axis=1
+            [cycle_wide[which, pl.ds(which * 8 + h * 4 + i, 32, stride=16), :] for h in range(2)], axis=1
         )
 
     for i in (0, 3, 1, 2):
@@ -632,20 +633,27 @@
     filter_terms(2)
     filter_terms(3)
     second_copy = core_send(2)
-    z_send(0)
+    fore_own = own_order(0, sem.at[38], sem.at[39], sem.at[40], sem.at[41])
     plane_send(1, first_copy)
+
+    degrees = pl.ds(pl.multiple_of((y_lo * 4 + b) * 48, 16), 48)
+    term = lax.dot_general(
+        spec[degrees, 0:256],
+        scaled_s[degrees, :],
+        (((0,), (0,)), ((), ())),
+        preferred_element_type=F32,
+    )
+    for h in range(2):
+        terms[h, 1024:1280, :] = term[:, h * 128 : h * 128 + 128]
+
+    spectral_copy = core_send(0)
+    plane_send(2, second_copy)
 
     def finish_output(i):
         fore = cycle_rows(0, i).astype(BF)
         spatial = jnp.dot(wide_ref[1, 16 : 16 + WIDTH, :], fore, preferred_element_type=F32)
         out_ref[i] = (hidden[i].astype(F32) + spatial.astype(BF).astype(F32)).astype(BF)
 
-    finish_output(0)
-    plane_send(2, second_copy)
-    finish_output(1)
-    gather_send(0)
-    finish_output(2)
-    finish_output(3)
     for copy in near_copies:
         copy.wait()
     for r in (0, 5):
@@ -669,15 +677,21 @@
 
     z_send(1)
     field_grad(0)
+    plane_send(0, spectral_copy)
     z_send(2)
     field_grad(1)
-    last_copies = [last_send(0)]
     gather_send(1)
+    z_send(0)
     field_grad(2)
     gather_send(2)
     field_grad(3)
-    last_copies.append(last_send(1))
+    gather_send(0)
+    last_copies = [last_send(1)]
+    wait_back(0, fore_own, sem.at[40])
+    for i in range(4):
+        finish_output(i)
     last_copies.append(last_send(2))
+    last_copies.append(last_send(0))
 
     whole_wait(side_size(field_wide), sem.at[0])
     whole_wait(lat_size(field_wide), sem.at[24])
@@ -687,8 +701,10 @@
     wait_partial(0, sem.at[7], None)
     whole_wait(table_buf.at[:, 0, 0, 0], sem.at[2])
     whole_wait(table_buf.at[pl.ds(0, 6), 0], sem.at[31])
-    whole_wait(mode_buf.at[pl.ds(0, 7)], sem.at[36])
-    whole_wait(cycle_buf.at[pl.ds(0, 16 * 31), :], sem.at[10])
+    whole_wait(mode_buf.at[0, pl.ds(0, 7)], sem.at[36])
+    whole_wait(mode_buf.at[0, pl.ds(0, 7)], sem.at[37])
+    whole_wait(cycle_buf.at[0, pl.ds(0, 16 * 31), :], sem.at[10])
+    whole_wait(cycle_buf.at[0, pl.ds(0, 16 * 31), :], sem.at[39])
     for n in range(3):
         whole_wait(plane_buf.at[plane_slots(n, 15)], sum_sem.at[n, 2])
         whole_wait(z_size(n), sum_sem.at[n, 4])
@@ -800,16 +816,16 @@
             pltpu.VMEM((3, 16, 128), BF),
             pltpu.VMEM((16, 32, 128), BF),
             pltpu.VMEM((8, 2, 2, 2, 32, 128), BF),
-            pltpu.VMEM((8, 2, 4, 16, 128), BF),
+            pltpu.VMEM((2, 8, 2, 4, 16, 128), BF),
             pltpu.VMEM((8, 2, 64, DEGREES), BF),
             pltpu.VMEM((DEGREES, 1024), BF),
             pltpu.VMEM((DEGREES, 256), F32),
             pltpu.VMEM((DEGREES, 512), BF),
             pltpu.VMEM((DEGREES, 256), BF),
             pltpu.VMEM((DEGREES, 512), BF),
-            pltpu.VMEM((512, 128), BF),
-            pltpu.VMEM((512, 128), BF),
-            pltpu.VMEM((512, 128), F32),
+            pltpu.VMEM((2, 512, 128), BF),
+            pltpu.VMEM((2, 512, 128), BF),
+            pltpu.VMEM((2, 512, 128), F32),
             pltpu.VMEM((6, 32, 256), BF),
             pltpu.VMEM((2, ROWS, 128), F32),
             pltpu.VMEM((ROWS, 128), BF),
@@ -817,7 +833,7 @@
             pltpu.VMEM((ROWS, 128), BF),
             pltpu.VMEM((15 * PIECE, 128), BF),
             pltpu.VMEM((8, PIECE, 128), BF),
-            dma((37,)),
+            dma((42,)),
             dma((1, 2, 3)),
             dma((4,)),
             dma((11,)),

time: 81.1 us -> 77.3 us (0.953)
  Pallas kernels: 78.7 us -> 75 us
    pallas_call x1, Pallas kernels: 76.2 us -> 72.4 us  [block_call(): pl.pallas_call(block_kernel, out_shape=(jax.ShapeDtypeStruct((4, WIDTH, 2...]
where the time goes in v3:
time: 77.3 us; the launch traced here: 77.1 us
  Pallas kernels  75 us (97%)
  local copies, waits for them, and re-layouts  1.5 us (2%)
    pallas_call x1, Pallas kernels, block_call(): pl.pallas_call(block_kernel, out_shape=(jax.ShapeDtypeStruct((4, WIDTH, 2...  72.4 us
    pallas_call x1, Pallas kernels, finish_call(): pl.pallas_call(finish_kernel, out_shape=(jax.ShapeDtypeStruct((4, WIDTH,...  2.52 us

profile of v3, /device:TPU:1, one launch (start us, length us, event | category | flops | bytes accessed | tf_op | source)
XLA Modules:
  0.0 77.1 jit_solution(1738878407535178543)
XLA Ops:
  0.6 0.8 %copy.19 = bf16[16,384,4]{1,0,2:T(8,128)(2,1)S(1)} copy(bf16[16,384,4]{1,2,0:T(4,128)(2,1)} %param.16) | data formatting | bytes 98304 | tf_op args[2]
  1.5 0.6 pad.4.legendre_ref
  2.1 72.4 %block.1 = (bf16[4,192,256]{2,1,0:T(8,128)(2,1)}, bf16[4,192,256]{2,1,0:T(8,128)(2,1)}, bf16[2,1280,128]{2,1,0:T(8,128)(2,1)}) custom-call(f32[4]{0:T(128)} %cycle_weight_ref.1, bf16[4,192,256]{2,1,0:T(8,128)(2,1)} %field_ref.1, bf16[4,192,256]{2,1,0:T(8,128)(2,1)} %cot_ref.1, bf16[16,16,128]{2,1,0:T(8,128)(2,1)} %pad.4.legendre_ref, ...), custom_call_target="tpu_custom_call" | custom-call | tf_op jit(solution)/shard_map/block/pallas_call | solution.py:784
  74.6 2.5 %finish.1 = (bf16[4,192,256]{2,1,0:T(8,128)(2,1)}, bf16[4,192,256]{2,1,0:T(8,128)(2,1)}, f32[1024,256]{1,0:T(8,128)}, f32[64,256]{1,0:T(8,128)}) custom-call(bf16[2,1280,128]{2,1,0:T(8,128)(2,1)} %get-tuple-element.11.sums_hbm, bf16[4,192,256]{2,1,0:T(8,128)(2,1)} %get-tuple-element.12.out_hbm, bf16[4,192,256]{2,1,0:T(8,128)(2,1)} %get-tuple-element.13.grad_hbm), custom_call_target="tpu_custom_call" | custom-call | tf_op jit(solution)/shard_map/finish/pallas_call | solution.py:754
  (3 shorter events, 0.1 us)

commit v4 on v3

--- a/solution.py
+++ b/solution.py
@@ -633,8 +633,8 @@
     filter_terms(2)
     filter_terms(3)
     second_copy = core_send(2)
+    plane_send(1, first_copy)
     fore_own = own_order(0, sem.at[38], sem.at[39], sem.at[40], sem.at[41])
-    plane_send(1, first_copy)
 
     degrees = pl.ds(pl.multiple_of((y_lo * 4 + b) * 48, 16), 48)
     term = lax.dot_general(

time: 77.3 us -> 74.9 us (0.969)
  Pallas kernels: 75 us -> 72.5 us
    pallas_call x1, Pallas kernels: 72.4 us -> 70 us  [block_call(): pl.pallas_call(block_kernel, out_shape=(jax.ShapeDtypeStruct((4, WIDTH, 2...]
where the time goes in v4:
time: 74.9 us; the launch traced here: 74.7 us
  Pallas kernels  72.5 us (97%)
  local copies, waits for them, and re-layouts  1.5 us (2%)
    pallas_call x1, Pallas kernels, block_call(): pl.pallas_call(block_kernel, out_shape=(jax.ShapeDtypeStruct((4, WIDTH, 2...  70 us
    pallas_call x1, Pallas kernels, finish_call(): pl.pallas_call(finish_kernel, out_shape=(jax.ShapeDtypeStruct((4, WIDTH,...  2.52 us

profile of v4, /device:TPU:1, one launch (start us, length us, event | category | flops | bytes accessed | tf_op | source)
XLA Modules:
  0.0 74.7 jit_solution(14533238610603070907)
XLA Ops:
  0.6 0.8 %copy.19 = bf16[16,384,4]{1,0,2:T(8,128)(2,1)S(1)} copy(bf16[16,384,4]{1,2,0:T(4,128)(2,1)} %param.16) | data formatting | bytes 98304 | tf_op args[2]
  1.5 0.6 pad.4.legendre_ref
  2.1 70.0 %block.1 = (bf16[4,192,256]{2,1,0:T(8,128)(2,1)}, bf16[4,192,256]{2,1,0:T(8,128)(2,1)}, bf16[2,1280,128]{2,1,0:T(8,128)(2,1)}) custom-call(f32[4]{0:T(128)} %cycle_weight_ref.1, bf16[4,192,256]{2,1,0:T(8,128)(2,1)} %field_ref.1, bf16[4,192,256]{2,1,0:T(8,128)(2,1)} %cot_ref.1, bf16[16,16,128]{2,1,0:T(8,128)(2,1)} %pad.4.legendre_ref, ...), custom_call_target="tpu_custom_call" | custom-call | tf_op jit(solution)/shard_map/block/pallas_call | solution.py:784
  72.2 2.5 %finish.1 = (bf16[4,192,256]{2,1,0:T(8,128)(2,1)}, bf16[4,192,256]{2,1,0:T(8,128)(2,1)}, f32[1024,256]{1,0:T(8,128)}, f32[64,256]{1,0:T(8,128)}) custom-call(bf16[2,1280,128]{2,1,0:T(8,128)(2,1)} %get-tuple-element.11.sums_hbm, bf16[4,192,256]{2,1,0:T(8,128)(2,1)} %get-tuple-element.12.out_hbm, bf16[4,192,256]{2,1,0:T(8,128)(2,1)} %get-tuple-element.13.grad_hbm), custom_call_target="tpu_custom_call" | custom-call | tf_op jit(solution)/shard_map/finish/pallas_call | solution.py:754
  (3 shorter events, 0.1 us)
